TPU v7x, 512 devices: a whole 4x8x8 slice. The times are simulated.
512 devices in a mesh: chan: 64 (over y_hi, z, core), tm: 8 (over y_lo, x).
Axes of the slice: x: 4, y: 8 (y_hi: 4, y_lo: 2; y = y_hi * 2 + y_lo), z: 8, core: 2. Of those that a mesh axis runs over, the one named last changes fastest.
Arguments:
- samples: bfloat16 [1024, 16384], P('chan', 'tm'), may hold values from -6 to 6
- fir_taps: float32 [96], replicated, may hold values from -0.625 to 0.625
- plan: int32 [4], replicated, may hold values from 1 to 63, as said below
Outputs:
- self_corr: float32 [1024, 16, 129], P(('chan', 'tm'))
- pair_corr: float32 [4, 1024, 16, 129], P(None, ('chan', 'tm'))
Inputs may be any that keep to these rules, and one draw needn't show every extreme that they name: Round r pairs block g with block g XOR plan[r]; the masks of the rounds are distinct, and the values 1 and 63 both occur.
All inputs are finite; a program needn't handle non-finite values.
Results may differ from a plain program's by a relative error of at most 0.0043.
Values may be sent and summed in bfloat16 or wider, within the bound.
A program may use at most 128 MiB of HBM per device.

v0:
```python
import math

import jax
import jax.numpy as jnp
from jax import lax
from jax.sharding import PartitionSpec as P

SEGS_DEV = 2
LAGS = 129
ROUNDS = 4


def shifted(x, axis, by):
    devices = lax.axis_size(axis)
    pairs = [(i, i + by) for i in range(devices) if 0 <= i + by < devices]
    return lax.ppermute(x, axis, pairs)


def from_partner(block, axis, distance):
    count = lax.axis_size(axis)
    route = []
    for low in range(count):
        high = low | 1 << distance
        if high != low and high < count:
            route += [(low, high), (high, low)]
    return lax.ppermute(block, axis, route)


def dft_matrix(length, half):
    sample_index = jnp.arange(length, dtype=jnp.int32)[:, None]
    freq_index = jnp.arange(half, dtype=jnp.int32)[None, :]
    angles = 2.0 * math.pi / length * (sample_index * freq_index % length).astype(jnp.float32)
    return jnp.concatenate([jnp.cos(angles), -jnp.sin(angles)], axis=1)


def band_matrix(fir_taps, seg_length):
    tap_count = fir_taps.shape[0]
    window = seg_length + tap_count - 1
    column = jnp.concatenate([fir_taps[::-1], jnp.zeros((window + 1 - tap_count,), jnp.float32)])
    tiled = jnp.tile(column, seg_length)[: seg_length * window]
    return tiled.reshape(seg_length, window).T


def whiten(filtered, matrix):
    spectrum = jnp.dot(
        filtered, matrix, precision=lax.Precision.HIGHEST, preferred_element_type=jnp.float32
    )
    half = matrix.shape[1] // 2
    real_part = spectrum[:, :half]
    imag_part = spectrum[:, half:]
    energy = real_part * real_part + imag_part * imag_part
    water_level = 0.1 * jnp.mean(energy, axis=1, keepdims=True)
    inverse_amp = lax.rsqrt(energy + water_level + 1e-06)
    return jnp.concatenate([real_part * inverse_amp, imag_part * inverse_amp], axis=1).astype(
        jnp.bfloat16
    )


def rotate(spectra, lag_count):
    half = spectra.shape[-1] // 2
    length = 2 * (half - 1)
    lag_value = jnp.arange(lag_count, dtype=jnp.int32) - lag_count // 2
    freq_index = jnp.arange(half, dtype=jnp.int32)
    angles = (
        2.0
        * math.pi
        / length
        * (lag_value[:, None] * freq_index[None, :] % length).astype(jnp.float32)
    )
    edges = (freq_index == 0) | (freq_index == half - 1)
    weight = jnp.where(edges, 1.0, 2.0).astype(jnp.float32) / length
    cosine = jnp.cos(angles) * weight
    sinus = jnp.sin(angles) * weight
    real_part = spectra[..., :half].astype(jnp.float32)[..., None, :]
    imag_part = spectra[..., half:].astype(jnp.float32)[..., None, :]
    rot_real = real_part * cosine - imag_part * sinus
    rot_imag = imag_part * cosine + real_part * sinus
    return jnp.concatenate([rot_real, rot_imag], axis=-1).astype(jnp.bfloat16)


def correlate(rotated, partner):
    return jnp.einsum("salk,sbk->abl", rotated, partner, preferred_element_type=jnp.float32)


def spectra_of(extended, fir_taps, matrix, seg_count, seg_length):
    tap_count = fir_taps.shape[0]
    window = seg_length + tap_count - 1
    chan_count = extended.shape[0]
    widened = extended.astype(jnp.float32)
    windows = jnp.stack(
        [widened[:, s * seg_length : s * seg_length + window] for s in range(seg_count)]
    )
    band = band_matrix(fir_taps, seg_length)
    filtered = jnp.dot(
        windows.reshape(seg_count * chan_count, window),
        band,
        precision=lax.Precision.HIGHEST,
        preferred_element_type=jnp.float32,
    )
    whitened = whiten(filtered, matrix)
    return whitened.reshape(seg_count, chan_count, matrix.shape[1])


def on_device(samples, fir_taps, plan):
    rim_width = fir_taps.shape[0] - 1
    record_length = samples.shape[1]
    seg_count = SEGS_DEV
    seg_length = record_length // seg_count
    before = shifted(samples[:, record_length - rim_width :], "tm", 1)
    extended = jnp.concatenate([before, samples], axis=1)
    matrix = dft_matrix(seg_length, seg_length // 2 + 1)
    own_spectra = spectra_of(extended, fir_taps, matrix, seg_count, seg_length)
    rotated = lax.map(lambda piece: rotate(piece, LAGS), own_spectra)
    self_term = correlate(rotated, own_spectra)
    bit_count = lax.axis_size("chan").bit_length() - 1
    self_corr = lax.psum_scatter(self_term, "tm", scatter_dimension=0, tiled=True)
    stacked = []
    for round_index in range(ROUNDS):
        round_mask = plan[round_index]
        partner = own_spectra
        for bit_index in range(bit_count):
            flag = round_mask >> bit_index & 1 == 1

            def hop_spectra(value, bit_index=bit_index):
                return from_partner(value, "chan", bit_index)

            partner = jnp.where(flag, hop_spectra(partner), partner)
        term = correlate(rotated, partner)
        stacked.append(lax.psum_scatter(term, "tm", scatter_dimension=0, tiled=True))
    pair_corr = jnp.stack(stacked)
    return (self_corr, pair_corr)


def solution(mesh):
    in_specs = (P("chan", "tm"), P(), P())
    out_specs = (P(("chan", "tm"), None, None), P(None, ("chan", "tm"), None, None))
    return jax.shard_map(
        on_device, mesh=mesh, in_specs=in_specs, out_specs=out_specs, check_vma=False
    )
```

profile of v0, /device:TPU:40, one launch (start us, length us, event | category | flops | bytes accessed | tf_op | source)
XLA Modules:
  0.0 402.7 jit_solution(2679480908318182421)
XLA Ops:
  7.2 0.0 reduce-scatter.14.cloned.1.call-start
  7.2 0.8 slice.42
  8.0 3.4 collective-permute-start
  11.4 11.3 %sine_negate_fusion = (f32[1024,513]{1,0:T(8,128)S(1)}, f32[1024,513]{1,0:T(8,128)}) fusion(), kind=kLoop, calls=%fused_computation.35 | loop fusion | flops 7879680 | bytes 4202496 | tf_op jit(solution)/shard_map/neg | solution.py:33
  22.7 0.1 rev.3
  22.8 2.5 tile.4
  25.3 6.4 %tile.10 = f32[1146880]{0:T(1024)} reshape(f32[1024,1120]{1,0:T(8,128)} %tile.4) | data formatting | bytes 9175040 | tf_op jit(solution)/shard_map/tile | solution.py:40
  31.7 3.9 slice.56
  35.6 8.4 %reshape.285 = f32[1024,1119]{1,0:T(8,128)} reshape(f32[1145856]{0:T(1024)} %slice.56) | data formatting | bytes 9166848 | tf_op jit(solution)/shard_map/reshape | solution.py:41
  44.0 0.1 maximum_convert_fusion
  44.1 6.8 %fusion.37 = f32[32,1024]{1,0:T(8,128)S(1)} fusion(f32[32,1119]{1,0:T(8,128)S(1)} %bitcast.99, f32[1024,1119]{1,0:T(8,128)} %reshape.285), kind=kOutput, calls=%fused_computation.92 | convolution fusion | flops 440008704 | bytes 4857728 | tf_op jit(solution)/shard_map/dot_general | solution.py:94
  51.0 2.8 fusion.10
  53.7 0.2 fusion.35
  53.9 0.1 multiply_convert_fusion.1
  54.1 0.1 pad_maximum_fusion.2
  54.2 1.9 collective-permute-start.1
  56.1 0.6 fusion.36
  71.5 0.1 broadcast_select_fusion.15
  71.6 4.3 %collective-permute-start.17 = (bf16[2,16,1026]{2,1,0:T(8,128)(2,1)S(1)}, bf16[2,16,1026]{2,1,0:T(8,128)(2,1)S(1)}, u32[]{:S(2)}, u32[]{:S(2)}) collective-permute-start(bf16[2,16,1026]{2,1,0:T(8,128)(2,1)S(1)} %get-tuple-element.61), channel_id=1, source_target_pairs={{0,16},{16,0},{8,24},{24,8},{32,48},{48,32},{40,56},{56,40},{64,80... | collective-permute-start | bytes 197000 | tf_op jit(solution)/shard_map/ppermute | solution.py:26
  75.9 14.9 %while.12 = (s32[]{:T(128)}, bf16[2,16,129,1026]{3,2,0,1:T(8,128)(2,1)}, bf16[2,16,1026]{2,1,0:T(8,128)(2,1)S(1)}, s32[]{:T(128)}) while((s32[]{:T(128)}, bf16[2,16,129,1026]{3,2,0,1:T(8,128)(2,1)}, bf16[2,16,1026]{2,1,0:T(8,128)(2,1)S(1)}, s32[]{:T(128)}) %tuple.48), condition=%wide.region_2.3_spmd, body=%wide.region_1.2_spmd.sunk | while | flops 18019256 | bytes 14778021 | solution.py:113
  76.2 1.4 cosine_multiply_fusion.2
  77.6 0.1 slice_convert_fusion.3
  77.7 1.7 fusion.48
  79.4 4.1 %fusion.49 = bf16[2,16,129,1026]{3,2,0,1:T(8,128)(2,1)} fusion(bf16[2,16,129,1026]{3,2,0,1:T(8,128)(2,1)} %get-tuple-element.108, s32[]{:T(128)S(6)} %copy.25, bf16[1,16,129,513]{3,2,1,0:T(8,128)(2,1)S(1)} %get-tuple-element.101, bf16[1,16,129,513]{3,2,1,0:T(8,128)(2,1)S(1)} %get-tuple-element.102), kind=kLoop, calls=%fused_computation.3.clone.1 | loop fusion | flops 8470656 | bytes 9248836 | tf_op jit(solution)/shard_map/while/body/jit(dynamic_update_index_in_dim)/dynamic_update_slice | solution.py:113
  83.5 1.4 cosine_multiply_fusion.2
  85.0 0.1 slice_convert_fusion.3
  85.1 1.7 fusion.48
  86.8 4.0 fusion.49
  90.8 1.9 collective-permute-start.12
  92.7 3.9 collective-permute-start.7
  96.6 1.9 collective-permute-start.2
  98.6 6.1 %collective-permute-start.18 = (bf16[2,16,1026]{2,1,0:T(8,128)(2,1)S(1)}, bf16[2,16,1026]{2,1,0:T(8,128)(2,1)S(1)}, u32[]{:S(2)}, u32[]{:S(2)}) collective-permute-start(bf16[2,16,1026]{2,1,0:T(8,128)(2,1)S(1)} %broadcast_select_fusion.1), channel_id=1, source_target_pairs={{0,32},{32,0},{8,40},{40,8},{16,48},{48,16},{24,56},{56,24},{64,96... | collective-permute-start | bytes 197000 | tf_op jit(solution)/shard_map/ppermute | solution.py:26
  104.7 1.9 collective-permute-start.13
  106.7 4.8 %collective-permute-start.8 = (bf16[2,16,1026]{2,1,0:T(8,128)(2,1)S(1)}, bf16[2,16,1026]{2,1,0:T(8,128)(2,1)S(1)}, u32[]{:S(2)}, u32[]{:S(2)}) collective-permute-start(bf16[2,16,1026]{2,1,0:T(8,128)(2,1)S(1)} %broadcast_select_fusion.11), channel_id=1, source_target_pairs={{0,32},{32,0},{8,40},{40,8},{16,48},{48,16},{24,56},{56,24},{64,96... | collective-permute-start | bytes 197000 | tf_op jit(solution)/shard_map/ppermute | solution.py:26
  111.6 1.9 collective-permute-start.3
  113.5 9.3 %collective-permute-start.19 = (bf16[2,16,1026]{2,1,0:T(8,128)(2,1)S(1)}, bf16[2,16,1026]{2,1,0:T(8,128)(2,1)S(1)}, u32[]{:S(2)}, u32[]{:S(2)}) collective-permute-start(bf16[2,16,1026]{2,1,0:T(8,128)(2,1)S(1)} %broadcast_select_fusion.2), channel_id=1, source_target_pairs={{0,64},{64,0},{8,72},{72,8},{16,80},{80,16},{24,88},{88,24},{32,96... | collective-permute-start | bytes 197000 | tf_op jit(solution)/shard_map/ppermute | solution.py:26
  122.8 1.9 collective-permute-start.14
  124.8 7.8 %collective-permute-start.9 = (bf16[2,16,1026]{2,1,0:T(8,128)(2,1)S(1)}, bf16[2,16,1026]{2,1,0:T(8,128)(2,1)S(1)}, u32[]{:S(2)}, u32[]{:S(2)}) collective-permute-start(bf16[2,16,1026]{2,1,0:T(8,128)(2,1)S(1)} %broadcast_select_fusion.12), channel_id=1, source_target_pairs={{0,64},{64,0},{8,72},{72,8},{16,80},{80,16},{24,88},{88,24},{32,96... | collective-permute-start | bytes 197000 | tf_op jit(solution)/shard_map/ppermute | solution.py:26
  132.7 1.9 collective-permute-start.4
  134.6 2.7 collective-permute-start.20
  137.4 4.0 %collective-permute-start.15 = (bf16[2,16,1026]{2,1,0:T(8,128)(2,1)S(1)}, bf16[2,16,1026]{2,1,0:T(8,128)(2,1)S(1)}, u32[]{:S(2)}, u32[]{:S(2)}) collective-permute-start(bf16[2,16,1026]{2,1,0:T(8,128)(2,1)S(1)} %broadcast_select_fusion.8), channel_id=1, source_target_pairs={{0,128},{128,0},{8,136},{136,8},{16,144},{144,16},{24,152},{152,24... | collective-permute-start | bytes 197000 | tf_op jit(solution)/shard_map/ppermute | solution.py:26
  141.5 2.7 collective-permute-start.10
  144.2 4.0 %collective-permute-start.5 = (bf16[2,16,1026]{2,1,0:T(8,128)(2,1)S(1)}, bf16[2,16,1026]{2,1,0:T(8,128)(2,1)S(1)}, u32[]{:S(2)}, u32[]{:S(2)}) collective-permute-start(bf16[2,16,1026]{2,1,0:T(8,128)(2,1)S(1)} %broadcast_select_fusion.18), channel_id=1, source_target_pairs={{0,128},{128,0},{8,136},{136,8},{16,144},{144,16},{24,152},{152,24... | collective-permute-start | bytes 197000 | tf_op jit(solution)/shard_map/ppermute | solution.py:26
  148.3 2.9 collective-permute-start.21
  151.2 6.8 %collective-permute-start.16 = (bf16[2,16,1026]{2,1,0:T(8,128)(2,1)S(1)}, bf16[2,16,1026]{2,1,0:T(8,128)(2,1)S(1)}, u32[]{:S(2)}, u32[]{:S(2)}) collective-permute-start(bf16[2,16,1026]{2,1,0:T(8,128)(2,1)S(1)} %broadcast_select_fusion.9), channel_id=1, source_target_pairs={{0,256},{256,0},{8,264},{264,8},{16,272},{272,16},{24,280},{280,24... | collective-permute-start | bytes 197000 | tf_op jit(solution)/shard_map/ppermute | solution.py:26
  158.1 2.9 collective-permute-start.11
  161.1 6.8 %collective-permute-start.6 = (bf16[2,16,1026]{2,1,0:T(8,128)(2,1)S(1)}, bf16[2,16,1026]{2,1,0:T(8,128)(2,1)S(1)}, u32[]{:S(2)}, u32[]{:S(2)}) collective-permute-start(bf16[2,16,1026]{2,1,0:T(8,128)(2,1)S(1)} %broadcast_select_fusion.19), channel_id=1, source_target_pairs={{0,256},{256,0},{8,264},{264,8},{16,272},{272,16},{24,280},{280,24... | collective-permute-start | bytes 197000 | tf_op jit(solution)/shard_map/ppermute | solution.py:26
  167.9 7.3 %convolution_bitcast_fusion = f32[16,16,129]{2,1,0:T(8,128)} fusion(bf16[2,16,129,1026]{3,2,0,1:T(8,128)(2,1)} %get-tuple-element.45, bf16[2,16,1026]{2,1,0:T(8,128)(2,1)S(1)} %collective-permute-done.21, bf16[2,16,1026]{2,1,0:T(8,128)(2,1)S(1)} %broadcast_select_fusion.4, pred[]{:T(512)} %bitcast.45), kind=kOutput, calls=%fused_computation.40 | convolution fusion | flops 135563328 | bytes 8734081 | tf_op jit(solution)/shard_map/salk,sbk->abl/dot_general | solution.py:82
  175.2 0.0 reduce-scatter.14.cloned.1.call-update
  175.2 0.0 reduce-scatter.12.cloned.1.call-start
  175.3 7.2 %convolution_bitcast_fusion.1 = f32[16,16,129]{2,1,0:T(8,128)} fusion(bf16[2,16,129,1026]{3,2,0,1:T(8,128)(2,1)} %get-tuple-element.45, bf16[2,16,1026]{2,1,0:T(8,128)(2,1)S(1)} %collective-permute-done.16, bf16[2,16,1026]{2,1,0:T(8,128)(2,1)S(1)} %broadcast_select_fusion.9, pred[]{:T(512)} %bitcast.34), kind=kOutput, calls=%fused_computation.41 | convolution fusion | flops 135563328 | bytes 8734081 | tf_op jit(solution)/shard_map/salk,sbk->abl/dot_general | solution.py:82
  182.5 0.0 reduce-scatter.12.cloned.1.call-update
  182.5 0.0 reduce-scatter.10.cloned.1.call-start
  182.6 7.3 %convolution_bitcast_fusion.2 = f32[16,16,129]{2,1,0:T(8,128)} fusion(bf16[2,16,129,1026]{3,2,0,1:T(8,128)(2,1)} %get-tuple-element.45, bf16[2,16,1026]{2,1,0:T(8,128)(2,1)S(1)} %collective-permute-done.11, bf16[2,16,1026]{2,1,0:T(8,128)(2,1)S(1)} %broadcast_select_fusion.14, pred[]{:T(512)} %bitcast.23), kind=kOutput, calls=%fused_computation.42 | convolution fusion | flops 135563328 | bytes 8734081 | tf_op jit(solution)/shard_map/salk,sbk->abl/dot_general | solution.py:82
  189.9 0.0 reduce-scatter.8.cloned.1.call-start
  189.9 7.3 %convolution_bitcast_fusion.3 = f32[16,16,129]{2,1,0:T(8,128)} fusion(bf16[2,16,129,1026]{3,2,0,1:T(8,128)(2,1)} %get-tuple-element.45, bf16[2,16,1026]{2,1,0:T(8,128)(2,1)S(1)} %collective-permute-done.6, bf16[2,16,1026]{2,1,0:T(8,128)(2,1)S(1)} %broadcast_select_fusion.19, pred[]{:T(512)} %bitcast.12), kind=kOutput, calls=%fused_computation.43 | convolution fusion | flops 135563328 | bytes 8734081 | tf_op jit(solution)/shard_map/salk,sbk->abl/dot_general | solution.py:82
  197.2 0.0 reduce-scatter.6.cloned.1.call-start
  197.3 7.3 %convolution_bitcast_fusion.4 = f32[16,16,129]{2,1,0:T(8,128)} fusion(bf16[2,16,129,1026]{3,2,0,1:T(8,128)(2,1)} %get-tuple-element.45, bf16[2,16,1026]{2,1,0:T(8,128)(2,1)S(1)} %get-tuple-element.121), kind=kOutput, calls=%fused_computation.44 | convolution fusion | flops 135530496 | bytes 8668416 | tf_op jit(solution)/shard_map/salk,sbk->abl/dot_general | solution.py:82
  204.6 14.1 %reduce-scatter.14.cloned.1.call-done = f32[2,16,129]{2,1,0:T(8,128)} async-done(((f32[16,16,129]{2,1,0:T(8,128)}), f32[2,16,129]{2,1,0:T(8,128)}) %reduce-scatter.14.cloned.1.call-update) | async-done | bytes 16528 | tf_op jit(solution)/shard_map/reduce_scatter | solution.py:129
  218.7 44.4 %reduce-scatter.12.cloned.1.call-done = f32[2,16,129]{2,1,0:T(8,128)} async-done(((f32[16,16,129]{2,1,0:T(8,128)}), f32[2,16,129]{2,1,0:T(8,128)}) %reduce-scatter.12.cloned.1.call-update) | async-done | bytes 16528 | tf_op jit(solution)/shard_map/reduce_scatter | solution.py:129
  263.1 44.2 %reduce-scatter.10.cloned.1.call-done = f32[2,16,129]{2,1,0:T(8,128)} async-done(((f32[16,16,129]{2,1,0:T(8,128)}), f32[2,16,129]{2,1,0:T(8,128)}) %reduce-scatter.10.cloned.1.call-update) | async-done | bytes 16528 | tf_op jit(solution)/shard_map/reduce_scatter | solution.py:129
  307.3 44.3 %reduce-scatter.8.cloned.1.call-done = f32[2,16,129]{2,1,0:T(8,128)} async-done(((f32[16,16,129]{2,1,0:T(8,128)}), f32[2,16,129]{2,1,0:T(8,128)}) %reduce-scatter.8.cloned.1.call-update) | async-done | bytes 16528 | tf_op jit(solution)/shard_map/reduce_scatter | solution.py:129
  351.6 1.5 pad_maximum_fusion.1
  353.1 43.1 %reduce-scatter.6.cloned.1.call-done = f32[2,16,129]{2,1,0:T(8,128)} async-done(((f32[16,16,129]{2,1,0:T(8,128)}), f32[2,16,129]{2,1,0:T(8,128)}) %reduce-scatter.6.cloned.1.call-update) | async-done | bytes 16528 | tf_op jit(solution)/shard_map/reduce_scatter | solution.py:116
  (60 shorter events, 0.4 us)
Async XLA Ops:
  7.2 15.5 %copy-start.3 = (f32[96]{0:T(128)S(1)}, f32[96]{0:T(128)}, u32[]{:S(2)}) copy-start(f32[96]{0:T(128)} %param.6) | copy-start | bytes 1156
  7.2 211.6 %reduce-scatter.14.cloned.1.call-start = ((), (), s32[]{:S(2)}) async-start(), calls=%async_computation.9 | async-start | bytes 294912 | tf_op jit(solution)/shard_map/reduce_scatter | solution.py:129
  8.0 36.0 %collective-permute-start = (bf16[16,95]{1,0:T(8,128)(2,1)S(1)}, bf16[16,95]{1,0:T(8,128)(2,1)S(1)}, u32[]{:S(2)}, u32[]{:S(2)}) collective-permute-start(bf16[16,95]{1,0:T(8,128)(2,1)S(1)} %slice.42), channel_id=1, source_target_pairs={{0,1},{1,2},{2,3},{3,4},{4,5},{5,6},{6,7},{8,9},{9,10},{10,11},{11... | collective-permute-start | bytes 9128 | tf_op jit(solution)/shard_map/ppermute | solution.py:16
  35.6 8.4 %copy-start.1 = (bf16[16,2048]{1,0:T(8,128)(2,1)S(1)}, bf16[16,2048]{1,0:T(8,128)(2,1)}, u32[]{:S(2)}) copy-start(bf16[16,2048]{1,0:T(8,128)(2,1)} %param.5) | copy-start | bytes 196612
  44.0 7.0 %copy-start = (f32[1024,513]{1,0:T(8,128)S(1)}, f32[1024,513]{1,0:T(8,128)}, u32[]{:S(2)}) copy-start(f32[1024,513]{1,0:T(8,128)} %get-tuple-element.71) | copy-start | bytes 6303748
  44.1 12.0 %copy-start.2 = (s32[4]{0:T(128)S(1)}, s32[4]{0:T(128)}, u32[]{:S(2)}) copy-start(s32[4]{0:T(128)} %param.7) | copy-start | bytes 52
  54.2 17.4 %collective-permute-start.1 = (bf16[2,16,1026]{2,1,0:T(8,128)(2,1)S(1)}, bf16[2,16,1026]{2,1,0:T(8,128)(2,1)S(1)}, u32[]{:S(2)}, u32[]{:S(2)}) collective-permute-start(bf16[2,16,1026]{2,1,0:T(8,128)(2,1)S(1)} %pad_maximum_fusion.2), channel_id=1, source_target_pairs={{0,8},{8,0},{16,24},{24,16},{32,40},{40,32},{48,56},{56,48},{64,72... | collective-permute-start | bytes 197000 | tf_op jit(solution)/shard_map/ppermute | solution.py:26
  71.6 26.9 %collective-permute-start.17 = (bf16[2,16,1026]{2,1,0:T(8,128)(2,1)S(1)}, bf16[2,16,1026]{2,1,0:T(8,128)(2,1)S(1)}, u32[]{:S(2)}, u32[]{:S(2)}) collective-permute-start(bf16[2,16,1026]{2,1,0:T(8,128)(2,1)S(1)} %get-tuple-element.61), channel_id=1, source_target_pairs={{0,16},{16,0},{8,24},{24,8},{32,48},{48,32},{40,56},{56,40},{64,80... | collective-permute-start | bytes 197000 | tf_op jit(solution)/shard_map/ppermute | solution.py:26
  90.8 13.9 %collective-permute-start.12 = (bf16[2,16,1026]{2,1,0:T(8,128)(2,1)S(1)}, bf16[2,16,1026]{2,1,0:T(8,128)(2,1)S(1)}, u32[]{:S(2)}, u32[]{:S(2)}) collective-permute-start(bf16[2,16,1026]{2,1,0:T(8,128)(2,1)S(1)} %get-tuple-element.62), channel_id=1, source_target_pairs={{0,16},{16,0},{8,24},{24,8},{32,48},{48,32},{40,56},{56,40},{64,80... | collective-permute-start | bytes 197000 | tf_op jit(solution)/shard_map/ppermute | solution.py:26
  92.7 14.0 %collective-permute-start.7 = (bf16[2,16,1026]{2,1,0:T(8,128)(2,1)S(1)}, bf16[2,16,1026]{2,1,0:T(8,128)(2,1)S(1)}, u32[]{:S(2)}, u32[]{:S(2)}) collective-permute-start(bf16[2,16,1026]{2,1,0:T(8,128)(2,1)S(1)} %get-tuple-element.63), channel_id=1, source_target_pairs={{0,16},{16,0},{8,24},{24,8},{32,48},{48,32},{40,56},{56,40},{64,80... | collective-permute-start | bytes 197000 | tf_op jit(solution)/shard_map/ppermute | solution.py:26
  96.6 14.9 %collective-permute-start.2 = (bf16[2,16,1026]{2,1,0:T(8,128)(2,1)S(1)}, bf16[2,16,1026]{2,1,0:T(8,128)(2,1)S(1)}, u32[]{:S(2)}, u32[]{:S(2)}) collective-permute-start(bf16[2,16,1026]{2,1,0:T(8,128)(2,1)S(1)} %get-tuple-element.60), channel_id=1, source_target_pairs={{0,16},{16,0},{8,24},{24,8},{32,48},{48,32},{40,56},{56,40},{64,80... | collective-permute-start | bytes 197000 | tf_op jit(solution)/shard_map/ppermute | solution.py:26
  98.6 14.9 %collective-permute-start.18 = (bf16[2,16,1026]{2,1,0:T(8,128)(2,1)S(1)}, bf16[2,16,1026]{2,1,0:T(8,128)(2,1)S(1)}, u32[]{:S(2)}, u32[]{:S(2)}) collective-permute-start(bf16[2,16,1026]{2,1,0:T(8,128)(2,1)S(1)} %broadcast_select_fusion.1), channel_id=1, source_target_pairs={{0,32},{32,0},{8,40},{40,8},{16,48},{48,16},{24,56},{56,24},{64,96... | collective-permute-start | bytes 197000 | tf_op jit(solution)/shard_map/ppermute | solution.py:26
  104.7 18.1 %collective-permute-start.13 = (bf16[2,16,1026]{2,1,0:T(8,128)(2,1)S(1)}, bf16[2,16,1026]{2,1,0:T(8,128)(2,1)S(1)}, u32[]{:S(2)}, u32[]{:S(2)}) collective-permute-start(bf16[2,16,1026]{2,1,0:T(8,128)(2,1)S(1)} %broadcast_select_fusion.6), channel_id=1, source_target_pairs={{0,32},{32,0},{8,40},{40,8},{16,48},{48,16},{24,56},{56,24},{64,96... | collective-permute-start | bytes 197000 | tf_op jit(solution)/shard_map/ppermute | solution.py:26
  106.7 18.1 %collective-permute-start.8 = (bf16[2,16,1026]{2,1,0:T(8,128)(2,1)S(1)}, bf16[2,16,1026]{2,1,0:T(8,128)(2,1)S(1)}, u32[]{:S(2)}, u32[]{:S(2)}) collective-permute-start(bf16[2,16,1026]{2,1,0:T(8,128)(2,1)S(1)} %broadcast_select_fusion.11), channel_id=1, source_target_pairs={{0,32},{32,0},{8,40},{40,8},{16,48},{48,16},{24,56},{56,24},{64,96... | collective-permute-start | bytes 197000 | tf_op jit(solution)/shard_map/ppermute | solution.py:26
  111.6 21.1 %collective-permute-start.3 = (bf16[2,16,1026]{2,1,0:T(8,128)(2,1)S(1)}, bf16[2,16,1026]{2,1,0:T(8,128)(2,1)S(1)}, u32[]{:S(2)}, u32[]{:S(2)}) collective-permute-start(bf16[2,16,1026]{2,1,0:T(8,128)(2,1)S(1)} %broadcast_select_fusion.16), channel_id=1, source_target_pairs={{0,32},{32,0},{8,40},{40,8},{16,48},{48,16},{24,56},{56,24},{64,96... | collective-permute-start | bytes 197000 | tf_op jit(solution)/shard_map/ppermute | solution.py:26
  113.5 21.1 %collective-permute-start.19 = (bf16[2,16,1026]{2,1,0:T(8,128)(2,1)S(1)}, bf16[2,16,1026]{2,1,0:T(8,128)(2,1)S(1)}, u32[]{:S(2)}, u32[]{:S(2)}) collective-permute-start(bf16[2,16,1026]{2,1,0:T(8,128)(2,1)S(1)} %broadcast_select_fusion.2), channel_id=1, source_target_pairs={{0,64},{64,0},{8,72},{72,8},{16,80},{80,16},{24,88},{88,24},{32,96... | collective-permute-start | bytes 197000 | tf_op jit(solution)/shard_map/ppermute | solution.py:26
  122.8 14.5 %collective-permute-start.14 = (bf16[2,16,1026]{2,1,0:T(8,128)(2,1)S(1)}, bf16[2,16,1026]{2,1,0:T(8,128)(2,1)S(1)}, u32[]{:S(2)}, u32[]{:S(2)}) collective-permute-start(bf16[2,16,1026]{2,1,0:T(8,128)(2,1)S(1)} %broadcast_select_fusion.7), channel_id=1, source_target_pairs={{0,64},{64,0},{8,72},{72,8},{16,80},{80,16},{24,88},{88,24},{32,96... | collective-permute-start | bytes 197000 | tf_op jit(solution)/shard_map/ppermute | solution.py:26
  124.8 16.6 %collective-permute-start.9 = (bf16[2,16,1026]{2,1,0:T(8,128)(2,1)S(1)}, bf16[2,16,1026]{2,1,0:T(8,128)(2,1)S(1)}, u32[]{:S(2)}, u32[]{:S(2)}) collective-permute-start(bf16[2,16,1026]{2,1,0:T(8,128)(2,1)S(1)} %broadcast_select_fusion.12), channel_id=1, source_target_pairs={{0,64},{64,0},{8,72},{72,8},{16,80},{80,16},{24,88},{88,24},{32,96... | collective-permute-start | bytes 197000 | tf_op jit(solution)/shard_map/ppermute | solution.py:26
  132.7 11.5 %collective-permute-start.4 = (bf16[2,16,1026]{2,1,0:T(8,128)(2,1)S(1)}, bf16[2,16,1026]{2,1,0:T(8,128)(2,1)S(1)}, u32[]{:S(2)}, u32[]{:S(2)}) collective-permute-start(bf16[2,16,1026]{2,1,0:T(8,128)(2,1)S(1)} %broadcast_select_fusion.17), channel_id=1, source_target_pairs={{0,64},{64,0},{8,72},{72,8},{16,80},{80,16},{24,88},{88,24},{32,96... | collective-permute-start | bytes 197000 | tf_op jit(solution)/shard_map/ppermute | solution.py:26
  134.6 13.6 %collective-permute-start.20 = (bf16[2,16,1026]{2,1,0:T(8,128)(2,1)S(1)}, bf16[2,16,1026]{2,1,0:T(8,128)(2,1)S(1)}, u32[]{:S(2)}, u32[]{:S(2)}) collective-permute-start(bf16[2,16,1026]{2,1,0:T(8,128)(2,1)S(1)} %broadcast_select_fusion.3), channel_id=1, source_target_pairs={{0,128},{128,0},{8,136},{136,8},{16,144},{144,16},{24,152},{152,24... | collective-permute-start | bytes 197000 | tf_op jit(solution)/shard_map/ppermute | solution.py:26
  137.4 13.8 %collective-permute-start.15 = (bf16[2,16,1026]{2,1,0:T(8,128)(2,1)S(1)}, bf16[2,16,1026]{2,1,0:T(8,128)(2,1)S(1)}, u32[]{:S(2)}, u32[]{:S(2)}) collective-permute-start(bf16[2,16,1026]{2,1,0:T(8,128)(2,1)S(1)} %broadcast_select_fusion.8), channel_id=1, source_target_pairs={{0,128},{128,0},{8,136},{136,8},{16,144},{144,16},{24,152},{152,24... | collective-permute-start | bytes 197000 | tf_op jit(solution)/shard_map/ppermute | solution.py:26
  141.5 16.6 %collective-permute-start.10 = (bf16[2,16,1026]{2,1,0:T(8,128)(2,1)S(1)}, bf16[2,16,1026]{2,1,0:T(8,128)(2,1)S(1)}, u32[]{:S(2)}, u32[]{:S(2)}) collective-permute-start(bf16[2,16,1026]{2,1,0:T(8,128)(2,1)S(1)} %broadcast_select_fusion.13), channel_id=1, source_target_pairs={{0,128},{128,0},{8,136},{136,8},{16,144},{144,16},{24,152},{152,24... | collective-permute-start | bytes 197000 | tf_op jit(solution)/shard_map/ppermute | solution.py:26
  144.2 16.8 %collective-permute-start.5 = (bf16[2,16,1026]{2,1,0:T(8,128)(2,1)S(1)}, bf16[2,16,1026]{2,1,0:T(8,128)(2,1)S(1)}, u32[]{:S(2)}, u32[]{:S(2)}) collective-permute-start(bf16[2,16,1026]{2,1,0:T(8,128)(2,1)S(1)} %broadcast_select_fusion.18), channel_id=1, source_target_pairs={{0,128},{128,0},{8,136},{136,8},{16,144},{144,16},{24,152},{152,24... | collective-permute-start | bytes 197000 | tf_op jit(solution)/shard_map/ppermute | solution.py:26
  148.3 19.6 %collective-permute-start.21 = (bf16[2,16,1026]{2,1,0:T(8,128)(2,1)S(1)}, bf16[2,16,1026]{2,1,0:T(8,128)(2,1)S(1)}, u32[]{:S(2)}, u32[]{:S(2)}) collective-permute-start(bf16[2,16,1026]{2,1,0:T(8,128)(2,1)S(1)} %broadcast_select_fusion.4), channel_id=1, source_target_pairs={{0,256},{256,0},{8,264},{264,8},{16,272},{272,16},{24,280},{280,24... | collective-permute-start | bytes 197000 | tf_op jit(solution)/shard_map/ppermute | solution.py:26
  151.2 24.0 %collective-permute-start.16 = (bf16[2,16,1026]{2,1,0:T(8,128)(2,1)S(1)}, bf16[2,16,1026]{2,1,0:T(8,128)(2,1)S(1)}, u32[]{:S(2)}, u32[]{:S(2)}) collective-permute-start(bf16[2,16,1026]{2,1,0:T(8,128)(2,1)S(1)} %broadcast_select_fusion.9), channel_id=1, source_target_pairs={{0,256},{256,0},{8,264},{264,8},{16,272},{272,16},{24,280},{280,24... | collective-permute-start | bytes 197000 | tf_op jit(solution)/shard_map/ppermute | solution.py:26
  158.1 24.5 %collective-permute-start.11 = (bf16[2,16,1026]{2,1,0:T(8,128)(2,1)S(1)}, bf16[2,16,1026]{2,1,0:T(8,128)(2,1)S(1)}, u32[]{:S(2)}, u32[]{:S(2)}) collective-permute-start(bf16[2,16,1026]{2,1,0:T(8,128)(2,1)S(1)} %broadcast_select_fusion.14), channel_id=1, source_target_pairs={{0,256},{256,0},{8,264},{264,8},{16,272},{272,16},{24,280},{280,24... | collective-permute-start | bytes 197000 | tf_op jit(solution)/shard_map/ppermute | solution.py:26
  161.1 28.9 %collective-permute-start.6 = (bf16[2,16,1026]{2,1,0:T(8,128)(2,1)S(1)}, bf16[2,16,1026]{2,1,0:T(8,128)(2,1)S(1)}, u32[]{:S(2)}, u32[]{:S(2)}) collective-permute-start(bf16[2,16,1026]{2,1,0:T(8,128)(2,1)S(1)} %broadcast_select_fusion.19), channel_id=1, source_target_pairs={{0,256},{256,0},{8,264},{264,8},{16,272},{272,16},{24,280},{280,24... | collective-permute-start | bytes 197000 | tf_op jit(solution)/shard_map/ppermute | solution.py:26
  175.2 87.9 %reduce-scatter.12.cloned.1.call-start = ((), (), s32[]{:S(2)}) async-start(), calls=%async_computation.8 | async-start | bytes 294912 | tf_op jit(solution)/shard_map/reduce_scatter | solution.py:129
  182.5 124.8 %reduce-scatter.10.cloned.1.call-start = ((), (), s32[]{:S(2)}) async-start(), calls=%async_computation.7 | async-start | bytes 294912 | tf_op jit(solution)/shard_map/reduce_scatter | solution.py:129
  189.9 161.7 %reduce-scatter.8.cloned.1.call-start = ((), (), s32[]{:S(2)}) async-start(), calls=%async_computation.6 | async-start | bytes 294912 | tf_op jit(solution)/shard_map/reduce_scatter | solution.py:129
  197.2 199.0 %reduce-scatter.6.cloned.1.call-start = ((), (), s32[]{:S(2)}) async-start(), calls=%async_computation.5 | async-start | bytes 294912 | tf_op jit(solution)/shard_map/reduce_scatter | solution.py:116
Sparse Core Ops, SparseCore 0:
  175.3 43.3 reduce-scatter.13
  221.7 41.3 reduce-scatter.11
  265.9 41.3 reduce-scatter.9
  310.2 41.3 reduce-scatter.7
  354.8 41.3 reduce-scatter.5
where the time goes:
time: 404 us; the launch traced here: 403 us
  waiting for transfers between devices  190 us (47%)
  starting transfers between devices  86.2 us (21%)
  matrix products  45.9 us (11%)
  between operations  29.1 us (7%)
  other arithmetic  28.2 us (7%)
  local copies, waits for them, and re-layouts  22.7 us (6%)
    reduce_scatter x4, waiting for transfers between devices, on_device(): lax.psum_scatter(term, 'tm', scatter_dimension=0, tiled=True)  147 us
    ppermute x21, starting transfers between devices, from_partner(): return lax.ppermute(block, axis, route)  82.6 us
    reduce_scatter x1, waiting for transfers between devices, on_device(): lax.psum_scatter(self_term, 'tm', scatter_dimension=0, tiled=True)  43.1 us
    dot_general x5, matrix products, correlate(): jnp.einsum('salk,sbk->abl', rotated, partner, preferred_element_type=jnp....  36.3 us
    neg x1, other arithmetic, dft_matrix(): return jnp.concatenate([jnp.cos(angles), -jnp.sin(angles)], axis=1)  11.3 us
    another operation x2, local copies, waits for them, and re-layouts, band_matrix(): tiled = jnp.tile(column, seg_length)[:seg_length * window]  8.92 us
    reshape x1, local copies, waits for them, and re-layouts, band_matrix(): return tiled.reshape(seg_length, window).T  8.35 us
    dynamic_update_slice x2, other arithmetic, on_device(): rotated = lax.map(lambda piece: rotate(piece, LAGS), own_spectra)  8.08 us
  transfers between devices with their start and end apart: 27, of which 5 were waited for; matrix products, arithmetic and copies ran while one was open for 21% of the time, Pallas kernels for 0%

commit v1 on v0

v1 whole, which is shorter than its diff:
```python
import functools

import jax
import jax.numpy as jnp
import ml_dtypes
import numpy as np
from jax import lax
from jax.experimental import pallas as pl
from jax.experimental.pallas import tpu as pltpu
from jax.sharding import PartitionSpec as P

MESH = pl.DeviceIdType.MESH
BF16 = jnp.bfloat16
F32 = jnp.float32

CH = 16
SEG = 1024
LAGS = 129
ROUNDS = 4
TM = 8
LANES = 128
TILES = 16
GROUPS = 4
HOP_CORE, HOP_Z1, HOP_Z2, HOP_Z6, HOP_Z7, HOP_Y1, HOP_Y3 = 1, 2, 4, 12, 14, 16, 48
CHAN_HOPS = (HOP_CORE, HOP_Z1, HOP_Z2, HOP_Z6, HOP_Z7, HOP_Y1, HOP_Y3)
STAGES = (
    (("A", HOP_Z1), ("B", HOP_Y1), ("F", HOP_Z7)),
    (("A", HOP_Z2), ("B", HOP_Y3)),
    (("A", HOP_Z6), ("B", HOP_Z1), ("F", HOP_Y3)),
    (("A", HOP_Y1), ("B", HOP_Z2)),
    (("A", HOP_Y3), ("B", HOP_Z6)),
)
MESSAGES = [(stage, name) for stage, hops in enumerate(STAGES) for name, _ in hops]


def group_frequencies():
    p = np.arange(64)
    first = np.concatenate([8 * p, 8 * p + 4])
    return [first] + [8 * np.arange(128) + q for q in (1, 2, 3)]


def split_bf16(x):
    high = x.astype(ml_dtypes.bfloat16)
    low = (x - high.astype(np.float64)).astype(ml_dtypes.bfloat16)
    return high, low


def dft_tables():
    r = np.arange(128)[:, None]
    tables = []
    for at, freqs in enumerate(group_frequencies()):
        angle = 2 * np.pi * ((r * freqs[None, :]) % SEG) / SEG
        cos, sin = np.cos(angle), np.sin(angle)
        if at == 0:
            top = np.concatenate([cos[:, :64], 0 * cos[:, 64:], -sin[:, :64], 0 * sin[:, 64:]], 1)
            top[:, 128] = (-1.0) ** np.arange(128)
            low = np.concatenate([0 * cos[:, :64], cos[:, 64:], 0 * sin[:, :64], -sin[:, 64:]], 1)
        else:
            top = np.concatenate([cos, -sin], 1)
            low = np.concatenate([sin, cos], 1)
        tables.append(np.concatenate([top, low], 0))
    return split_bf16(np.stack(tables))


def lag_table():
    lags = np.arange(LAGS) - LAGS // 2
    rows = []
    for at, freqs in enumerate(group_frequencies()):
        angle = 2 * np.pi * ((freqs[:, None] * lags[None, :]) % SEG) / SEG
        re, im = np.cos(angle) * 2 / SEG, -np.sin(angle) * 2 / SEG
        if at == 0:
            re[0] = 1 / SEG
            im[0] = (-1.0) ** np.abs(lags) / SEG
        rows += [re, im]
    table = np.zeros((GROUPS * 256, 256))
    table[:, :LAGS] = np.concatenate(rows, 0)
    return table.astype(ml_dtypes.bfloat16)


def kernel(
    plan, samples, taps, dft_high, dft_low, lag_mat, self_out, pair_out,
    core_body, hop_body, hold, own_tail, core_tail, hop_tail, hold_tail, send_tail,
    band, xr, xi, yr, yi, yr2, cross, parts, inbox,
    core_sem, tail_sem, ctail_sem, body_sem, htail_sem, red_sem, here_sem,
):
    c = lax.axis_index("chan")
    t = lax.axis_index("tm")

    def chan_peer(hop):
        return (lax.bitwise_xor(c, jnp.int32(hop)), t)

    def tm_peer(d):
        return (c, lax.bitwise_xor(t, jnp.int32(d)))

    barrier = pltpu.get_barrier_semaphore()
    for hop in CHAN_HOPS:
        pl.semaphore_signal(barrier, inc=1, device_id=chan_peer(hop), device_id_type=MESH)
    for d in range(1, TM):
        pl.semaphore_signal(barrier, inc=1, device_id=tm_peer(d), device_id_type=MESH)

    p = [plan[r] for r in range(ROUNDS)]
    free = [jnp.logical_and(m != 1, m != 63) for m in p]
    mask_a = jnp.where(free[0], p[0], jnp.where(free[1], p[1], p[2]))
    mask_b = p[0] + p[1] + p[2] + p[3] - 64 - mask_a

    def flag(m, hop):
        bit = lambda k: (m >> k) & 1
        if hop == HOP_CORE:
            v = bit(0)
        elif hop == HOP_Z1:
            v = bit(1)
        elif hop == HOP_Z6:
            v = bit(3)
        elif hop == HOP_Z2:
            v = bit(2) ^ bit(3)
        elif hop == HOP_Y3:
            v = bit(5)
        else:
            v = bit(4) ^ bit(5)
        return v == 1

    masks = {"A": mask_a, "B": mask_b}

    rolled = pltpu.roll(jnp.broadcast_to(taps[...], (256, 256)), 128, 1, stride=1, stride_axis=0)
    toeplitz = rolled[:, :LANES]
    high = toeplitz.astype(BF16)
    band[:, :LANES] = high
    band[:, LANES:] = (toeplitz - high.astype(F32)).astype(BF16)

    pl.semaphore_wait(barrier, len(CHAN_HOPS) + TM - 1)

    def remote(src, dst, sem, device):
        return pltpu.make_async_remote_copy(
            src_ref=src, dst_ref=dst, send_sem=sem.at[0], recv_sem=sem.at[1],
            device_id=device, device_id_type=MESH,
        )

    core_copy = remote(samples, core_body, core_sem, chan_peer(HOP_CORE))
    core_copy.start()
    send_tail[...] = samples[:, (TILES - 1) * LANES :]
    tail_copy = remote(send_tail, own_tail, tail_sem, (c, lax.rem(t + 1, TM)))
    tail_copy.start()

    body_copies, tail_copies = {}, {}

    def send_bodies(stage):
        for name, hop in STAGES[stage]:
            at = MESSAGES.index((stage, name))
            src = core_body if (stage, name) == (0, "F") else hold.at[at]
            copy = remote(src, hop_body.at[at], body_sem.at[at], chan_peer(hop))
            copy.start()
            body_copies[at] = copy

    def send_tails(stage):
        for name, hop in STAGES[stage]:
            at = MESSAGES.index((stage, name))
            copy = remote(hold_tail.at[at], hop_tail.at[at], htail_sem.at[at], chan_peer(hop))
            copy.start()
            tail_copies[at] = copy

    def last_message(name, stage):
        return [i for i, (s, n) in enumerate(MESSAGES) if n == name and s <= stage][-1]

    def advance(stage, copies, held, arrived):
        later = {}
        for name, hop in STAGES[stage]:
            at = MESSAGES.index((stage, name))
            copies[at].wait_recv()
            if name == "F":
                later[name] = arrived[at]
            else:
                later[name] = jnp.where(flag(masks[name], hop), arrived[at], held[at])
        return later

    def place(values, stage, held):
        for name, value in values.items():
            following = [i for i, (s, n) in enumerate(MESSAGES) if n == name and s > stage]
            slot = following[0] if following else len(MESSAGES) + "ABF".index(name)
            held[slot] = value

    def spectra(body, tail):
        tiles = [body[:, j * LANES : (j + 1) * LANES] for j in range(TILES)]
        now = jnp.concatenate(tiles, 0)
        before = jnp.concatenate([tail] + tiles[:-1], 0)
        both = jnp.dot(jnp.concatenate([before, now], 1), band[...], preferred_element_type=F32)
        filtered = both[:, :LANES] + both[:, LANES:]
        y = []
        for j in range(8):
            y.append(jnp.concatenate(
                [filtered[(s * 8 + j) * CH : (s * 8 + j + 1) * CH] for s in range(2)], 0))
        add = [y[j] + y[j + 4] for j in range(4)]
        sub = [y[j] - y[j + 4] for j in range(4)]
        root = np.float32(np.sqrt(0.5))
        e02, e13 = add[0] + add[2], add[1] + add[3]
        dm, dp = (sub[1] - sub[3]) * root, (sub[1] + sub[3]) * root
        z = (
            (e02 + e13, e02 - e13),
            (sub[0] + dm, -sub[2] - dp),
            (add[0] - add[2], add[3] - add[1]),
            (sub[0] - dm, sub[2] - dp),
        )
        re, im = [], []
        total = None
        for g in range(GROUPS):
            full = jnp.concatenate(z[g], 1)
            z_high = full.astype(BF16)
            z_low = (full - z_high.astype(F32)).astype(BF16)
            first = jnp.dot(jnp.concatenate([z_high, z_low], 0), dft_high[g], preferred_element_type=F32)
            second = jnp.dot(z_high, dft_low[g], preferred_element_type=F32)
            out = first[:32] + (first[32:] + second)
            re.append(out[:, :LANES])
            im.append(out[:, LANES:])
            energy = re[g] * re[g] + im[g] * im[g]
            total = energy if total is None else total + energy
        water = jnp.sum(total, axis=1, keepdims=True) * np.float32(0.1 / 513) + np.float32(1e-6)
        lane0 = lax.broadcasted_iota(jnp.int32, (32, LANES), 1) == 0
        result = []
        for g in range(GROUPS):
            re2, im2 = re[g] * re[g], im[g] * im[g]
            if g == 0:
                inv_re = lax.rsqrt(jnp.where(lane0, re2, re2 + im2) + water)
                inv_im = lax.rsqrt(jnp.where(lane0, im2, re2 + im2) + water)
            else:
                inv_re = inv_im = lax.rsqrt(re2 + im2 + water)
            result.append((
                (re[g] * inv_re).astype(BF16).astype(F32),
                (im[g] * inv_im).astype(BF16).astype(F32),
            ))
        return result

    def keep_partner(spec):
        lane0 = lax.broadcasted_iota(jnp.int32, (32, LANES), 1) == 0
        for g in range(GROUPS):
            re, im = spec[g]
            yr[g] = re
            if g == 0:
                yi[g] = jnp.where(lane0, 0.0, im)
                yr2[g] = jnp.where(lane0, im, re)
            else:
                yi[g] = im
                yr2[g] = re

    def correlate(slot):
        def step(a, carry):
            for g in range(GROUPS):
                sum_re = sum_im = None
                for s in range(2):
                    rows = pl.ds(s * CH, CH)
                    x_re = xr[g, pl.ds(s * CH + a, 1), :]
                    x_im = xi[g, pl.ds(s * CH + a, 1), :]
                    y_im = yi[g, rows, :]
                    term_re = x_re * yr[g, rows, :] + x_im * y_im
                    term_im = x_im * yr2[g, rows, :] - x_re * y_im
                    sum_re = term_re if s == 0 else sum_re + term_re
                    sum_im = term_im if s == 0 else sum_im + term_im
                where = pl.ds(pl.multiple_of(a * CH, CH), CH)
                cross[where, g * 256 : g * 256 + LANES] = sum_re.astype(BF16)
                cross[where, g * 256 + LANES : (g + 1) * 256] = sum_im.astype(BF16)
            return carry

        lax.fori_loop(0, CH, step, 0)
        lagged = jnp.dot(cross[...], lag_mat[...], preferred_element_type=F32)
        parts[slot] = lagged.astype(BF16).reshape(TM, 32, 256)

    reduce_copies = []

    def send_parts(first, count):
        for d in range(1, TM):
            copy = remote(
                parts.at[pl.ds(first, count), lax.bitwise_xor(t, jnp.int32(d))],
                inbox.at[d - 1, pl.ds(first, count)],
                red_sem.at[first, d - 1],
                tm_peer(d),
            )
            copy.start()
            reduce_copies.append(copy)

    core_copy.wait_recv()
    mine, theirs = samples[...], core_body[...]
    place({n: jnp.where(flag(masks[n], HOP_CORE), theirs, mine) for n in "AB"}, -1, hold)
    send_bodies(0)

    tail_copy.wait_recv()
    own_tail[...] = jnp.where(t == 0, jnp.zeros_like(own_tail), own_tail[...])
    core_tail_copy = remote(own_tail, core_tail, ctail_sem, chan_peer(HOP_CORE))
    core_tail_copy.start()

    spec = spectra(mine, own_tail[...])
    for g in range(GROUPS):
        xr[g], xi[g] = spec[g]
    keep_partner(spec)

    core_tail_copy.wait_recv()
    mine, theirs = own_tail[...], core_tail[...]
    values = {n: jnp.where(flag(masks[n], HOP_CORE), theirs, mine) for n in "AB"}
    values["F"] = theirs
    place(values, -1, hold_tail)
    send_tails(0)

    correlate(0)

    def hop_on(stage):
        place(advance(stage, body_copies, hold, hop_body), stage, hold)
        if stage + 1 < len(STAGES):
            send_bodies(stage + 1)
        place(advance(stage, tail_copies, hold_tail, hop_tail), stage, hold_tail)
        if stage + 1 < len(STAGES):
            send_tails(stage + 1)

    hop_on(0)
    keep_partner(spectra(core_body[...], core_tail[...]))
    correlate(1)
    send_parts(0, 2)
    hop_on(1)
    hop_on(2)
    at = len(MESSAGES) + 2
    keep_partner(spectra(hold[at], hold_tail[at]))
    correlate(2)
    send_parts(2, 1)
    hop_on(3)
    hop_on(4)
    for i in range(2):
        at = len(MESSAGES) + i
        keep_partner(spectra(hold[at], hold_tail[at]))
        correlate(3 + i)
        send_parts(3 + i, 1)

    for copy in [core_copy, tail_copy, core_tail_copy, *body_copies.values(), *tail_copies.values()]:
        copy.wait_send()
    for copy in reduce_copies:
        copy.wait_recv()
    sums = []
    for slot in range(5):
        acc = parts[slot, t].astype(F32)
        for d in range(1, TM):
            acc = acc + inbox[d - 1, slot].astype(F32)
        sums.append(acc[:, :LAGS].reshape(2, CH, LAGS))
    self_out[...] = sums[0]
    for r in range(ROUNDS):
        rest = jnp.where(p[r] == mask_a, sums[3], sums[4])
        pair_out[r] = jnp.where(p[r] == 1, sums[1], jnp.where(p[r] == 63, sums[2], rest))
    for copy in reduce_copies:
        copy.wait_send()


def on_device(samples, fir_taps, plan):
    dft_high, dft_low = dft_tables()
    lag_mat = lag_table()
    taps = jnp.pad(fir_taps, (0, 256 - fir_taps.shape[0])).reshape(1, 256)
    vmem = pl.BlockSpec(memory_space=pltpu.VMEM)
    slots = len(MESSAGES) + 3
    n = len(MESSAGES)
    dma = pltpu.SemaphoreType.DMA
    return pl.pallas_call(
        kernel,
        out_shape=(
            jax.ShapeDtypeStruct((2, CH, LAGS), F32),
            jax.ShapeDtypeStruct((ROUNDS, 2, CH, LAGS), F32),
        ),
        in_specs=[pl.BlockSpec(memory_space=pltpu.SMEM)] + [vmem] * 5,
        out_specs=(vmem, vmem),
        scratch_shapes=[
            pltpu.VMEM((CH, 2048), BF16),
            pltpu.VMEM((n, CH, 2048), BF16),
            pltpu.VMEM((slots, CH, 2048), BF16),
            pltpu.VMEM((CH, LANES), BF16),
            pltpu.VMEM((CH, LANES), BF16),
            pltpu.VMEM((n, CH, LANES), BF16),
            pltpu.VMEM((slots, CH, LANES), BF16),
            pltpu.VMEM((CH, LANES), BF16),
            pltpu.VMEM((256, 256), BF16),
            pltpu.VMEM((GROUPS, 32, LANES), F32),
            pltpu.VMEM((GROUPS, 32, LANES), F32),
            pltpu.VMEM((GROUPS, 32, LANES), F32),
            pltpu.VMEM((GROUPS, 32, LANES), F32),
            pltpu.VMEM((GROUPS, 32, LANES), F32),
            pltpu.VMEM((256, GROUPS * 256), BF16),
            pltpu.VMEM((5, TM, 32, 256), BF16),
            pltpu.VMEM((TM - 1, 5, 32, 256), BF16),
            dma((2,)),
            dma((2,)),
            dma((2,)),
            dma((n, 2)),
            dma((n, 2)),
            dma((5, TM - 1, 2)),
            pltpu.SemaphoreType.REGULAR,
        ],
        compiler_params=pltpu.CompilerParams(
            collective_id=0, has_side_effects=True, vmem_limit_bytes=48 * 1024 * 1024
        ),
        cost_estimate=pl.CostEstimate(flops=10**9, bytes_accessed=4 * 10**6, transcendentals=10**5),
        name="correlate_blocks",
    )(plan, samples, taps, jnp.asarray(dft_high), jnp.asarray(dft_low), jnp.asarray(lag_mat))


def solution(mesh):
    in_specs = (P("chan", "tm"), P(), P())
    out_specs = (P(("chan", "tm"), None, None), P(None, ("chan", "tm"), None, None))
    return jax.shard_map(
        on_device, mesh=mesh, in_specs=in_specs, out_specs=out_specs, check_vma=False
    )
```

time: 404 us -> 56.5 us (0.14)
  the two profiles are of different devices: /device:TPU:40 before, /device:TPU:72 now
where the time goes in v1:
time: 56.5 us; the launch traced here: 56.2 us
  Pallas kernels  49 us (87%)
  local copies, waits for them, and re-layouts  6.55 us (12%)
  between operations  0.64 us (1%)
    pallas_call x1, Pallas kernels, on_device(): pl.pallas_call(kernel, out_shape=(jax.ShapeDtypeStruct((2, CH, LAGS), F32...  49 us
    unnamed x12, local copies, waits for them, and re-layouts  5.89 us

profile of v1, /device:TPU:72, one launch (start us, length us, event | category | flops | bytes accessed | tf_op | source)
XLA Modules:
  0.0 56.2 jit_solution(7851881975454953183)
XLA Ops:
  0.6 0.7 %pad.4 = f32[256]{0:T(256)S(1)} pad(f32[96]{0:T(128)} %param.7, f32[]{:T(128)} %constant.8.clone.1), padding=0_160 | pad | bytes 1412 | tf_op jit(solution)/shard_map/jit(_pad)/pad | solution.py:349
  1.3 0.0 copy-start.1
  1.3 0.7 %copy-done.1 = s32[4]{0:T(128)S(1)} copy-done((s32[4]{0:T(128)S(1)}, s32[4]{0:T(128)}, u32[]{:S(2)}) %copy-start.1) | copy-done | bytes 40
  1.9 0.0 copy-start
  1.9 0.8 %copy-done = bf16[16,2048]{1,0:T(8,128)(2,1)S(1)} copy-done((bf16[16,2048]{1,0:T(8,128)(2,1)S(1)}, bf16[16,2048]{1,0:T(8,128)(2,1)}, u32[]{:S(2)}) %copy-start) | copy-done | bytes 65560
  2.8 0.0 copy-start.2
  2.8 1.0 %copy-done.2 = bf16[1024,256]{1,0:T(8,128)(2,1)S(1)} copy-done((bf16[1024,256]{1,0:T(8,128)(2,1)S(1)}, bf16[1024,256]{1,0:T(8,128)(2,1)}, u32[]{:S(2)}) %copy-start.2) | copy-done | bytes 524312
  3.8 0.0 copy-start.3
  3.8 1.0 %copy-done.3 = bf16[4,256,256]{2,1,0:T(8,128)(2,1)S(1)} copy-done((bf16[4,256,256]{2,1,0:T(8,128)(2,1)S(1)}, bf16[4,256,256]{2,1,0:T(8,128)(2,1)}, u32[]{:S(2)}) %copy-start.3) | copy-done | bytes 524312
  4.9 0.0 copy-start.4
  4.9 1.0 %copy-done.4 = bf16[4,256,256]{2,1,0:T(8,128)(2,1)S(1)} copy-done((bf16[4,256,256]{2,1,0:T(8,128)(2,1)S(1)}, bf16[4,256,256]{2,1,0:T(8,128)(2,1)}, u32[]{:S(2)}) %copy-start.4) | copy-done | bytes 524312
  5.9 49.0 %correlate_blocks.1 = (f32[2,16,129]{2,1,0:T(8,128)S(1)}, f32[4,2,16,129]{3,2,1,0:T(8,128)S(1)}) custom-call(s32[4]{0:T(128)S(1)} %copy-done.1, bf16[16,2048]{1,0:T(8,128)(2,1)S(1)} %copy-done, f32[1,256]{1,0:T(1,128)S(1)} %bitcast.1, bf16[4,256,256]{2,1,0:T(8,128)(2,1)S(1)} %copy-done.4, bf16[4,256,256]{2,1,0:T(8,128)(2,1)S(1)} %copy-done.3, ...), custom_call_target="tpu_custom_call" | custom-call | flops 1000000000 | bytes 4000000 | tf_op jit(solution)/shard_map/correlate_blocks/pallas_call | solution.py:354
  54.9 0.6 %copy.10 = f32[2,16,129]{2,1,0:T(8,128)} copy(f32[2,16,129]{2,1,0:T(8,128)S(1)} %get-tuple-element.4) | data formatting | bytes 33024
  55.5 0.7 %copy.11 = f32[4,2,16,129]{3,2,1,0:T(8,128)} copy(f32[4,2,16,129]{3,2,1,0:T(8,128)S(1)} %get-tuple-element.5) | data formatting | bytes 132096
Async XLA Ops:
  1.3 0.7 %copy-start.1 = (s32[4]{0:T(128)S(1)}, s32[4]{0:T(128)}, u32[]{:S(2)}) copy-start(s32[4]{0:T(128)} %plan.1) | copy-start | bytes 52
  1.9 0.8 %copy-start = (bf16[16,2048]{1,0:T(8,128)(2,1)S(1)}, bf16[16,2048]{1,0:T(8,128)(2,1)}, u32[]{:S(2)}) copy-start(bf16[16,2048]{1,0:T(8,128)(2,1)} %samples.1) | copy-start | bytes 196612
  2.8 1.0 %copy-start.2 = (bf16[1024,256]{1,0:T(8,128)(2,1)S(1)}, bf16[1024,256]{1,0:T(8,128)(2,1)}, u32[]{:S(2)}) copy-start(bf16[1024,256]{1,0:T(8,128)(2,1)} %constant.11.clone.lag_mat) | copy-start | bytes 1572868
  3.8 1.0 %copy-start.3 = (bf16[4,256,256]{2,1,0:T(8,128)(2,1)S(1)}, bf16[4,256,256]{2,1,0:T(8,128)(2,1)}, u32[]{:S(2)}) copy-start(bf16[4,256,256]{2,1,0:T(8,128)(2,1)} %constant.10.clone.dft_low) | copy-start | bytes 1572868
  4.9 1.0 %copy-start.4 = (bf16[4,256,256]{2,1,0:T(8,128)(2,1)S(1)}, bf16[4,256,256]{2,1,0:T(8,128)(2,1)}, u32[]{:S(2)}) copy-start(bf16[4,256,256]{2,1,0:T(8,128)(2,1)} %constant.9.clone.dft_high) | copy-start | bytes 1572868

commit v2 on v1

v2 whole, which is shorter than its diff:
```python
import functools

import jax
import jax.numpy as jnp
import ml_dtypes
import numpy as np
from jax import lax
from jax.experimental import pallas as pl
from jax.experimental.pallas import tpu as pltpu
from jax.sharding import PartitionSpec as P

MESH = pl.DeviceIdType.MESH
BF16 = jnp.bfloat16
F32 = jnp.float32

CH = 16
SEG = 1024
LAGS = 129
ROUNDS = 4
TM = 8
LANES = 128
TILES = 16
CHUNKS = 4
WIDTH = 2048 // CHUNKS
GROUPS = 4
HOP_CORE, HOP_Z1, HOP_Z2, HOP_Z6, HOP_Z7, HOP_Y1, HOP_Y3 = 1, 2, 4, 12, 14, 16, 48
CHAN_HOPS = (HOP_CORE, HOP_Z1, HOP_Z2, HOP_Z6, HOP_Z7, HOP_Y1, HOP_Y3)
STAGES = (
    (("A", HOP_Z1), ("B", HOP_Y1)),
    (("A", HOP_Z2), ("B", HOP_Y3), ("F", HOP_Z7)),
    (("A", HOP_Z6), ("B", HOP_Z1), ("F", HOP_Y3)),
    (("A", HOP_Y1), ("B", HOP_Z2)),
    (("A", HOP_Y3), ("B", HOP_Z6)),
)
MESSAGES = [(stage, name) for stage, hops in enumerate(STAGES) for name, _ in hops]
FIRST_F = [m for m in MESSAGES if m[1] == "F"][0]


def group_frequencies():
    p = np.arange(64)
    first = np.concatenate([8 * p, 8 * p + 4])
    return [first] + [8 * np.arange(128) + q for q in (1, 2, 3)]


def split_bf16(x):
    high = x.astype(ml_dtypes.bfloat16)
    low = (x - high.astype(np.float64)).astype(ml_dtypes.bfloat16)
    return high, low


def dft_tables():
    r = np.arange(128)[:, None]
    tables = []
    for at, freqs in enumerate(group_frequencies()):
        angle = 2 * np.pi * ((r * freqs[None, :]) % SEG) / SEG
        cos, sin = np.cos(angle), np.sin(angle)
        if at == 0:
            top = np.concatenate([cos[:, :64], 0 * cos[:, 64:], -sin[:, :64], 0 * sin[:, 64:]], 1)
            top[:, 128] = (-1.0) ** np.arange(128)
            low = np.concatenate([0 * cos[:, :64], cos[:, 64:], 0 * sin[:, :64], -sin[:, 64:]], 1)
        else:
            top = np.concatenate([cos, -sin], 1)
            low = np.concatenate([sin, cos], 1)
        tables.append(np.concatenate([top, low], 0))
    return split_bf16(np.stack(tables))


def lag_table():
    lags = np.arange(LAGS) - LAGS // 2
    rows = []
    for at, freqs in enumerate(group_frequencies()):
        angle = 2 * np.pi * ((freqs[:, None] * lags[None, :]) % SEG) / SEG
        re, im = np.cos(angle) * 2 / SEG, -np.sin(angle) * 2 / SEG
        if at == 0:
            re[0] = 1 / SEG
            im[0] = (-1.0) ** np.abs(lags) / SEG
        rows += [re, im]
    table = np.zeros((GROUPS * 256, 256))
    table[:, :LAGS] = np.concatenate(rows, 0)
    return table.astype(ml_dtypes.bfloat16)


def known(mask):
    return jnp.logical_or(mask == 1, mask == 63)


def kernel(
    plan_in, samples, taps_in, dft_high_in, dft_low_in, lag_in, sums,
    plan, taps, taps_row, dft_high, dft_low, lag_mat, own_body, core_body, hop_body, hold,
    own_tail, core_tail, hop_tail, hold_tail,
    band, xr, xi, yr, yi, yr2, cross, parts, inbox,
    load_sem, core_sem, tail_sem, body_sem, htail_sem, red_sem,
):
    c = lax.axis_index("chan")
    t = lax.axis_index("tm")

    def chan_peer(hop):
        return (lax.bitwise_xor(c, jnp.int32(hop)), t)

    def tm_peer(d):
        return (c, lax.bitwise_xor(t, jnp.int32(d)))

    later, earlier = lax.rem(t + 1, TM), lax.rem(t + TM - 1, TM)
    other = lax.bitwise_xor(c, jnp.int32(HOP_CORE))

    barrier = pltpu.get_barrier_semaphore()
    greeted = [chan_peer(hop) for hop in CHAN_HOPS] + [tm_peer(d) for d in range(1, TM)]
    greeted += [(other, later), (other, earlier)]
    for device in greeted:
        pl.semaphore_signal(barrier, inc=1, device_id=device, device_id_type=MESH)

    loads = [
        pltpu.make_async_copy(src, dst, load_sem.at[i])
        for i, (src, dst) in enumerate((
            (plan_in, plan), (taps_in, taps), (samples, own_body),
            (dft_high_in, dft_high), (dft_low_in, dft_low), (lag_in, lag_mat),
        ))
    ]
    for load in loads:
        load.start()
    loads[0].wait()
    loads[1].wait()

    p = [plan[r] for r in range(ROUNDS)]
    mask_a = jnp.where(known(p[0]), jnp.where(known(p[1]), p[2], p[1]), p[0])
    mask_b = p[0] + p[1] + p[2] + p[3] - 64 - mask_a
    masks = {"A": mask_a, "B": mask_b}

    def flag(m, hop):
        bit = lambda k: (m >> k) & 1
        if hop == HOP_CORE:
            v = bit(0)
        elif hop == HOP_Z1:
            v = bit(1)
        elif hop == HOP_Z6:
            v = bit(3)
        elif hop == HOP_Z2:
            v = bit(2) ^ bit(3)
        elif hop == HOP_Y3:
            v = bit(5)
        else:
            v = bit(4) ^ bit(5)
        return v == 1

    taps_row[...] = jnp.zeros_like(taps_row)
    taps_row[:, : taps.shape[1]] = taps[...]
    rolled = pltpu.roll(jnp.broadcast_to(taps_row[...], (256, 256)), 128, 1, stride=1, stride_axis=0)
    toeplitz = rolled[:, :LANES]
    high = toeplitz.astype(BF16)
    band[:, :LANES] = high
    band[:, LANES:] = (toeplitz - high.astype(F32)).astype(BF16)
    loads[2].wait()

    pl.semaphore_wait(barrier, len(greeted))

    def remote(src, dst, sem, device):
        return pltpu.make_async_remote_copy(
            src_ref=src, dst_ref=dst, send_sem=sem.at[0], recv_sem=sem.at[1],
            device_id=device, device_id_type=MESH,
        )

    def lanes(h):
        return slice(h * WIDTH, (h + 1) * WIDTH)

    core_copies = []
    for h in range(CHUNKS):
        copy = remote(own_body.at[:, lanes(h)], core_body.at[:, lanes(h)], core_sem.at[h], chan_peer(HOP_CORE))
        copy.start()
        core_copies.append(copy)
    end = own_body.at[:, (TILES - 1) * LANES :]
    tail_copies = [
        remote(end, own_tail, tail_sem.at[0], (c, later)),
        remote(end, core_tail, tail_sem.at[1], (other, later)),
    ]
    for copy in tail_copies:
        copy.start()

    body_hops, tail_hops = {}, {}
    finals = {"A": len(MESSAGES), "B": len(MESSAGES) + 1, "F": len(MESSAGES) + 2}

    def next_slot(name, stage):
        following = [i for i, (s, n) in enumerate(MESSAGES) if n == name and s > stage]
        return following[0] if following else finals[name]

    def send_body(at, h):
        if at < len(MESSAGES):
            stage, name = MESSAGES[at]
            src = core_body if (stage, name) == FIRST_F else hold.at[at]
            copy = remote(
                src.at[:, lanes(h)], hop_body.at[at, :, lanes(h)], body_sem.at[at, h],
                chan_peer(dict(STAGES[stage])[name]),
            )
            copy.start()
            body_hops[at, h] = copy

    def send_tail(at):
        if at < len(MESSAGES):
            stage, name = MESSAGES[at]
            copy = remote(
                hold_tail.at[at], hop_tail.at[at], htail_sem.at[at], chan_peer(dict(STAGES[stage])[name])
            )
            copy.start()
            tail_hops[at] = copy

    def hop_bodies(stage):
        for h in range(CHUNKS):
            for name, hop in STAGES[stage]:
                at = MESSAGES.index((stage, name))
                slot = next_slot(name, stage)
                body_hops[at, h].wait_recv()
                value = hop_body[at, :, lanes(h)]
                if name != "F":
                    value = jnp.where(flag(masks[name], hop), value, hold[at, :, lanes(h)])
                hold[slot, :, lanes(h)] = value
                send_body(slot, h)

    def hop_tails(stage):
        for name, hop in STAGES[stage]:
            at = MESSAGES.index((stage, name))
            slot = next_slot(name, stage)
            tail_hops[at].wait_recv()
            value = hop_tail[at]
            if name != "F":
                value = jnp.where(flag(masks[name], hop), value, hold_tail[at])
            hold_tail[slot] = value
            send_tail(slot)

    def spectra(blocks):
        filtered = []
        for body, tail in blocks:
            tiles = [body[:, j * LANES : (j + 1) * LANES] for j in range(TILES)]
            now = jnp.concatenate(tiles, 0)
            before = jnp.concatenate([tail] + tiles[:-1], 0)
            both = jnp.dot(jnp.concatenate([before, now], 1), band[...], preferred_element_type=F32)
            filtered.append(both[:, :LANES] + both[:, LANES:])
        y = []
        for j in range(8):
            y.append(jnp.concatenate(
                [f[(s * 8 + j) * CH : (s * 8 + j + 1) * CH] for f in filtered for s in range(2)], 0))
        count = 32 * len(blocks)
        add = [y[j] + y[j + 4] for j in range(4)]
        sub = [y[j] - y[j + 4] for j in range(4)]
        root = np.float32(np.sqrt(0.5))
        e02, e13 = add[0] + add[2], add[1] + add[3]
        dm, dp = (sub[1] - sub[3]) * root, (sub[1] + sub[3]) * root
        z = (
            (e02 + e13, e02 - e13),
            (sub[0] + dm, -sub[2] - dp),
            (add[0] - add[2], add[3] - add[1]),
            (sub[0] - dm, sub[2] - dp),
        )
        re, im = [], []
        total = None
        for g in range(GROUPS):
            full = jnp.concatenate(z[g], 1)
            z_high = full.astype(BF16)
            z_low = (full - z_high.astype(F32)).astype(BF16)
            first = jnp.dot(jnp.concatenate([z_high, z_low], 0), dft_high[g], preferred_element_type=F32)
            second = jnp.dot(z_high, dft_low[g], preferred_element_type=F32)
            out = first[:count] + (first[count:] + second)
            re.append(out[:, :LANES])
            im.append(out[:, LANES:])
            energy = re[g] * re[g] + im[g] * im[g]
            total = energy if total is None else total + energy
        water = jnp.sum(total, axis=1, keepdims=True) * np.float32(0.1 / 513) + np.float32(1e-6)
        lane0 = lax.broadcasted_iota(jnp.int32, (count, LANES), 1) == 0
        result = []
        for g in range(GROUPS):
            re2, im2 = re[g] * re[g], im[g] * im[g]
            if g == 0:
                inv_re = lax.rsqrt(jnp.where(lane0, re2, re2 + im2) + water)
                inv_im = lax.rsqrt(jnp.where(lane0, im2, re2 + im2) + water)
            else:
                inv_re = inv_im = lax.rsqrt(re2 + im2 + water)
            result.append((
                (re[g] * inv_re).astype(BF16).astype(F32),
                (im[g] * inv_im).astype(BF16).astype(F32),
            ))
        return result

    def keep_partner(spec, block):
        rows = slice(block * 32, block * 32 + 32)
        lane0 = lax.broadcasted_iota(jnp.int32, (32, LANES), 1) == 0
        for g in range(GROUPS):
            re, im = spec[g][0][rows], spec[g][1][rows]
            yr[g] = re
            if g == 0:
                yi[g] = jnp.where(lane0, 0.0, im)
                yr2[g] = jnp.where(lane0, im, re)
            else:
                yi[g] = im
                yr2[g] = re

    def correlate(slot):
        def step(a, carry):
            for g in range(GROUPS):
                sum_re = sum_im = None
                for s in range(2):
                    rows = pl.ds(s * CH, CH)
                    x_re = xr[g, pl.ds(s * CH + a, 1), :]
                    x_im = xi[g, pl.ds(s * CH + a, 1), :]
                    y_im = yi[g, rows, :]
                    term_re = x_re * yr[g, rows, :] + x_im * y_im
                    term_im = x_im * yr2[g, rows, :] - x_re * y_im
                    sum_re = term_re if s == 0 else sum_re + term_re
                    sum_im = term_im if s == 0 else sum_im + term_im
                where = pl.ds(pl.multiple_of(a * CH, CH), CH)
                cross[where, g * 256 : g * 256 + LANES] = sum_re.astype(BF16)
                cross[where, g * 256 + LANES : (g + 1) * 256] = sum_im.astype(BF16)
            return carry

        lax.fori_loop(0, CH, step, 0)
        lagged = jnp.dot(cross[...], lag_mat[...], preferred_element_type=F32)
        parts[slot] = lagged.astype(BF16).reshape(TM, 32, 256)

    reduce_copies = []

    def send_parts(first, count):
        for d in range(1, TM):
            copy = remote(
                parts.at[pl.ds(first, count), lax.bitwise_xor(t, jnp.int32(d))],
                inbox.at[d - 1, pl.ds(first, count)],
                red_sem.at[first, d - 1],
                tm_peer(d),
            )
            copy.start()
            reduce_copies.append(copy)

    for h in range(CHUNKS):
        core_copies[h].wait_recv()
        mine, theirs = own_body[:, lanes(h)], core_body[:, lanes(h)]
        for n in "AB":
            at = next_slot(n, -1)
            hold[at, :, lanes(h)] = jnp.where(flag(masks[n], HOP_CORE), theirs, mine)
            send_body(at, h)
        send_body(next_slot("F", -1), h)
    for load in loads[3:]:
        load.wait()

    hop_bodies(0)
    for copy in tail_copies:
        copy.wait_recv()
    mine = jnp.where(t == 0, jnp.zeros_like(own_tail), own_tail[...])
    theirs = jnp.where(t == 0, jnp.zeros_like(core_tail), core_tail[...])
    for n in "ABF":
        at = next_slot(n, -1)
        hold_tail[at] = theirs if n == "F" else jnp.where(flag(masks[n], HOP_CORE), theirs, mine)
        send_tail(at)
    spec = spectra([(own_body[...], mine), (core_body[...], theirs)])
    for g in range(GROUPS):
        xr[g], xi[g] = spec[g][0][:32], spec[g][1][:32]
    keep_partner(spec, 0)
    correlate(0)
    hop_tails(0)
    hop_bodies(1)
    keep_partner(spec, 1)
    correlate(1)
    send_parts(0, 2)
    hop_tails(1)
    hop_bodies(2)
    hop_tails(2)
    spec = spectra([(hold[finals["F"]], hold_tail[finals["F"]])])
    keep_partner(spec, 0)
    correlate(2)
    send_parts(2, 1)
    hop_bodies(3)
    hop_tails(3)
    hop_bodies(4)
    hop_tails(4)
    spec = spectra([(hold[finals[n]], hold_tail[finals[n]]) for n in "AB"])
    for i in range(2):
        keep_partner(spec, i)
        correlate(3 + i)
        send_parts(3 + i, 1)

    for copy in [*core_copies, *tail_copies, *body_hops.values(), *tail_hops.values()]:
        copy.wait_send()
    for copy in reduce_copies:
        copy.wait_recv()
    for slot in range(5):
        acc = parts[slot, t].astype(F32)
        for d in range(1, TM):
            acc = acc + inbox[d - 1, slot].astype(F32)
        sums[slot] = acc
    for copy in reduce_copies:
        copy.wait_send()


def hand_out(plan, sums, self_out, pair_out):
    p = [plan[r] for r in range(ROUNDS)]
    first = jnp.where(known(p[0]), jnp.where(known(p[1]), p[2], p[1]), p[0])
    shaped = lambda i: sums[i][:, :LAGS].reshape(2, CH, LAGS)
    self_out[...] = shaped(0)
    for r in range(ROUNDS):
        slot = jnp.where(p[r] == 1, 1, jnp.where(p[r] == 63, 2, jnp.where(p[r] == first, 3, 4)))
        pair_out[r] = shaped(slot)


def on_device(samples, fir_taps, plan):
    dft_high, dft_low = dft_tables()
    lag_mat = lag_table()
    vmem = pl.BlockSpec(memory_space=pltpu.VMEM)
    anywhere = pl.BlockSpec(memory_space=pl.ANY)
    n = len(MESSAGES)
    slots = n + 3
    dma = pltpu.SemaphoreType.DMA
    taps = fir_taps.reshape(1, -1)
    sums = pl.pallas_call(
        kernel,
        out_shape=jax.ShapeDtypeStruct((5, 32, 256), F32),
        in_specs=[anywhere] * 6,
        out_specs=vmem,
        scratch_shapes=[
            pltpu.SMEM((ROUNDS,), jnp.int32),
            pltpu.VMEM(taps.shape, F32),
            pltpu.VMEM((1, 256), F32),
            pltpu.VMEM(dft_high.shape, BF16),
            pltpu.VMEM(dft_low.shape, BF16),
            pltpu.VMEM(lag_mat.shape, BF16),
            pltpu.VMEM((CH, 2048), BF16),
            pltpu.VMEM((CH, 2048), BF16),
            pltpu.VMEM((n, CH, 2048), BF16),
            pltpu.VMEM((slots, CH, 2048), BF16),
            pltpu.VMEM((CH, LANES), BF16),
            pltpu.VMEM((CH, LANES), BF16),
            pltpu.VMEM((n, CH, LANES), BF16),
            pltpu.VMEM((slots, CH, LANES), BF16),
            pltpu.VMEM((256, 256), BF16),
            pltpu.VMEM((GROUPS, 32, LANES), F32),
            pltpu.VMEM((GROUPS, 32, LANES), F32),
            pltpu.VMEM((GROUPS, 32, LANES), F32),
            pltpu.VMEM((GROUPS, 32, LANES), F32),
            pltpu.VMEM((GROUPS, 32, LANES), F32),
            pltpu.VMEM((256, GROUPS * 256), BF16),
            pltpu.VMEM((5, TM, 32, 256), BF16),
            pltpu.VMEM((TM - 1, 5, 32, 256), BF16),
            dma((6,)),
            dma((CHUNKS, 2)),
            dma((2, 2)),
            dma((n, CHUNKS, 2)),
            dma((n, 2)),
            dma((5, TM - 1, 2)),
        ],
        compiler_params=pltpu.CompilerParams(
            collective_id=0, has_side_effects=True, vmem_limit_bytes=62 * 1024 * 1024
        ),
        cost_estimate=pl.CostEstimate(flops=10**9, bytes_accessed=4 * 10**6, transcendentals=10**5),
        name="correlate_blocks",
    )(plan, samples, taps, jnp.asarray(dft_high), jnp.asarray(dft_low), jnp.asarray(lag_mat))
    return pl.pallas_call(
        hand_out,
        out_shape=(
            jax.ShapeDtypeStruct((2, CH, LAGS), F32),
            jax.ShapeDtypeStruct((ROUNDS, 2, CH, LAGS), F32),
        ),
        in_specs=[pl.BlockSpec(memory_space=pltpu.SMEM), vmem],
        out_specs=(vmem, vmem),
        cost_estimate=pl.CostEstimate(flops=0, bytes_accessed=5 * 10**5, transcendentals=0),
        name="hand_out_rounds",
    )(plan, sums)


def solution(mesh):
    in_specs = (P("chan", "tm"), P(), P())
    out_specs = (P(("chan", "tm"), None, None), P(None, ("chan", "tm"), None, None))
    return jax.shard_map(
        on_device, mesh=mesh, in_specs=in_specs, out_specs=out_specs, check_vma=False
    )
```

time: 56.5 us -> 49.2 us (0.87)
  the two profiles are of different devices: /device:TPU:72 before, /device:TPU:8 now
where the time goes in v2:
time: 49.2 us; the launch traced here: 49 us
  Pallas kernels  48.4 us (98%)
  between operations  0.64 us (1%)
    pallas_call x1, Pallas kernels, on_device(): pl.pallas_call(kernel, out_shape=jax.ShapeDtypeStruct((5, 32, 256), F32),...  46.8 us
    pallas_call x1, Pallas kernels, on_device(): pl.pallas_call(hand_out, out_shape=(jax.ShapeDtypeStruct((2, CH, LAGS), F...  1.6 us

profile of v2, /device:TPU:8, one launch (start us, length us, event | category | flops | bytes accessed | tf_op | source)
XLA Modules:
  0.0 49.0 jit_solution(2449772071296141073)
XLA Ops:
  0.6 46.8 %correlate_blocks.1.sums = f32[5,32,256]{2,1,0:T(8,128)} custom-call(s32[4]{0:T(128)} %plan.1, bf16[16,2048]{1,0:T(8,128)(2,1)} %samples.1, f32[1,96]{1,0:T(1,128)} %bitcast.1, bf16[4,256,256]{2,1,0:T(8,128)(2,1)} %constant.6.clone.dft_high_in, bf16[4,256,256]{2,1,0:T(8,128)(2,1)} %constant.7.clone.dft_low_in, bf16[1024,256]{1,0:T(8,128)(2,1)} %constant.8.clone.lag_in), custom_call_target="tpu_custom_call" | custom-call | flops 1000000000 | bytes 4000000 | tf_op jit(solution)/shard_map/correlate_blocks/pallas_call | solution.py:408
  47.4 1.6 %hand_out_rounds.1 = (f32[2,16,129]{2,1,0:T(8,128)}, f32[4,2,16,129]{3,2,1,0:T(8,128)}) custom-call(s32[4]{0:T(128)} %plan.1, f32[5,32,256]{2,1,0:T(8,128)} %correlate_blocks.1.sums), custom_call_target="tpu_custom_call" | custom-call | bytes 500000 | tf_op jit(solution)/shard_map/hand_out_rounds/pallas_call | solution.py:450

commit v3 on v2

--- a/solution.py
+++ b/solution.py
@@ -22,18 +22,22 @@
 TILES = 16
 CHUNKS = 4
 WIDTH = 2048 // CHUNKS
+ROWS = 48
 GROUPS = 4
 HOP_CORE, HOP_Z1, HOP_Z2, HOP_Z6, HOP_Z7, HOP_Y1, HOP_Y3 = 1, 2, 4, 12, 14, 16, 48
-CHAN_HOPS = (HOP_CORE, HOP_Z1, HOP_Z2, HOP_Z6, HOP_Z7, HOP_Y1, HOP_Y3)
+CHAN_HOPS = (HOP_CORE, HOP_Z1, HOP_Z1 ^ HOP_CORE, HOP_Z2, HOP_Z6, HOP_Z7, HOP_Y1, HOP_Y3)
 STAGES = (
-    (("A", HOP_Z1), ("B", HOP_Y1)),
     (("A", HOP_Z2), ("B", HOP_Y3), ("F", HOP_Z7)),
-    (("A", HOP_Z6), ("B", HOP_Z1), ("F", HOP_Y3)),
-    (("A", HOP_Y1), ("B", HOP_Z2)),
-    (("A", HOP_Y3), ("B", HOP_Z6)),
+    (("A", HOP_Z6), ("B", HOP_Y1), ("F", HOP_Y3)),
+    (("A", HOP_Y1), ("B", HOP_Z6)),
+    (("A", HOP_Y3), ("B", HOP_Z2)),
 )
-MESSAGES = [(stage, name) for stage, hops in enumerate(STAGES) for name, _ in hops]
-FIRST_F = [m for m in MESSAGES if m[1] == "F"][0]
+FLAGGED = (HOP_CORE, HOP_Z1, HOP_Z2, HOP_Z6, HOP_Y1, HOP_Y3)
+NEAR = (HOP_CORE, HOP_Z1, HOP_Z1 ^ HOP_CORE)
+
+
+def messages(stages):
+    return [(stage, name, hop) for stage, hops in enumerate(stages) for name, hop in hops]
 
 
 def group_frequencies():
@@ -77,6 +81,7 @@
         rows += [re, im]
     table = np.zeros((GROUPS * 256, 256))
     table[:, :LAGS] = np.concatenate(rows, 0)
+    table[:, LAGS] = table[:, LAGS - 1]
     return table.astype(ml_dtypes.bfloat16)
 
 
@@ -84,12 +89,47 @@
     return jnp.logical_or(mask == 1, mask == 63)
 
 
+class Stream:
+    def __init__(self, stages, pieces, flags, held, arrived, sems, send):
+        self.pieces, self.flags = pieces, flags
+        self.held, self.arrived, self.sems, self.send = held, arrived, sems, send
+        self.order = messages(stages)
+        self.finals = {n: len(self.order) + k for k, n in enumerate("ABF")}
+        self.copies = {}
+
+    def slot(self, name, stage=-1):
+        following = [k for k, (at, n, _) in enumerate(self.order) if n == name and at > stage]
+        return following[0] if following else self.finals[name]
+
+    def leave(self, at, h, source=None):
+        if at < len(self.order):
+            piece = self.pieces[h]
+            source = self.held.at[at] if source is None else source
+            copy = self.send(
+                source.at[:, piece], self.arrived.at[at, :, piece], self.sems.at[at, h], self.order[at][2]
+            )
+            copy.start()
+            self.copies[at, h] = copy
+
+    def hop(self, stage):
+        for h, piece in enumerate(self.pieces):
+            for at, (when, name, hop) in enumerate(self.order):
+                if when == stage:
+                    self.copies[at, h].wait_recv()
+                    value = self.arrived[at, :, piece]
+                    if name != "F":
+                        value = jnp.where(self.flags[name, hop], value, self.held[at, :, piece])
+                    after = self.slot(name, stage)
+                    self.held[after, :, piece] = value
+                    self.leave(after, h)
+
+
 def kernel(
     plan_in, samples, taps_in, dft_high_in, dft_low_in, lag_in, sums,
-    plan, taps, taps_row, dft_high, dft_low, lag_mat, own_body, core_body, hop_body, hold,
-    own_tail, core_tail, hop_tail, hold_tail,
+    plan, taps, taps_row, dft_high, dft_low, lag_mat, own, near_body, hop_body, hold,
+    near_tails, hop_tail, hold_tail,
     band, xr, xi, yr, yi, yr2, cross, parts, inbox,
-    load_sem, core_sem, tail_sem, body_sem, htail_sem, red_sem,
+    load_sem, first_sem, near_sem, body_sem, tail_sem, red_sem,
 ):
     c = lax.axis_index("chan")
     t = lax.axis_index("tm")
@@ -101,30 +141,52 @@
         return (c, lax.bitwise_xor(t, jnp.int32(d)))
 
     later, earlier = lax.rem(t + 1, TM), lax.rem(t + TM - 1, TM)
-    other = lax.bitwise_xor(c, jnp.int32(HOP_CORE))
 
     barrier = pltpu.get_barrier_semaphore()
     greeted = [chan_peer(hop) for hop in CHAN_HOPS] + [tm_peer(d) for d in range(1, TM)]
-    greeted += [(other, later), (other, earlier)]
+    greeted += [(chan_peer(hop)[0], side) for hop in NEAR for side in (later, earlier)]
     for device in greeted:
         pl.semaphore_signal(barrier, inc=1, device_id=device, device_id_type=MESH)
 
     loads = [
         pltpu.make_async_copy(src, dst, load_sem.at[i])
         for i, (src, dst) in enumerate((
-            (plan_in, plan), (taps_in, taps), (samples, own_body),
+            (plan_in, plan), (taps_in, taps), (samples, own),
             (dft_high_in, dft_high), (dft_low_in, dft_low), (lag_in, lag_mat),
         ))
     ]
     for load in loads:
         load.start()
+    pl.semaphore_wait(barrier, len(greeted))
+
+    def remote(src, dst, sem, device):
+        return pltpu.make_async_remote_copy(
+            src_ref=src, dst_ref=dst, send_sem=sem.at[0], recv_sem=sem.at[1],
+            device_id=device, device_id_type=MESH,
+        )
+
+    def by_hop(src, dst, sem, hop):
+        return remote(src, dst, sem, chan_peer(hop))
+
+    pieces = [slice(h * WIDTH, (h + 1) * WIDTH) for h in range(CHUNKS)]
+    first_copies = [
+        [by_hop(samples.at[:, piece], near_body.at[k, :, piece], first_sem.at[h, k], hop) for k, hop in enumerate(NEAR)]
+        for h, piece in enumerate(pieces)
+    ]
+    end = samples.at[:, (TILES - 1) * LANES :]
+    near_copies = [
+        remote(end, near_tails.at[k], near_sem.at[k], (chan_peer(hop)[0], later))
+        for k, hop in enumerate((0,) + NEAR)
+    ]
+    for copy in [*first_copies[0], *near_copies, *sum(first_copies[1:], [])]:
+        copy.start()
+
     loads[0].wait()
     loads[1].wait()
 
     p = [plan[r] for r in range(ROUNDS)]
     mask_a = jnp.where(known(p[0]), jnp.where(known(p[1]), p[2], p[1]), p[0])
     mask_b = p[0] + p[1] + p[2] + p[3] - 64 - mask_a
-    masks = {"A": mask_a, "B": mask_b}
 
     def flag(m, hop):
         bit = lambda k: (m >> k) & 1
@@ -142,6 +204,8 @@
             v = bit(4) ^ bit(5)
         return v == 1
 
+    flags = {(n, hop): flag(m, hop) for n, m in (("A", mask_a), ("B", mask_b)) for hop in FLAGGED}
+
     taps_row[...] = jnp.zeros_like(taps_row)
     taps_row[:, : taps.shape[1]] = taps[...]
     rolled = pltpu.roll(jnp.broadcast_to(taps_row[...], (256, 256)), 128, 1, stride=1, stride_axis=0)
@@ -149,88 +213,19 @@
     high = toeplitz.astype(BF16)
     band[:, :LANES] = high
     band[:, LANES:] = (toeplitz - high.astype(F32)).astype(BF16)
-    loads[2].wait()
-
-    pl.semaphore_wait(barrier, len(greeted))
-
-    def remote(src, dst, sem, device):
-        return pltpu.make_async_remote_copy(
-            src_ref=src, dst_ref=dst, send_sem=sem.at[0], recv_sem=sem.at[1],
-            device_id=device, device_id_type=MESH,
-        )
-
-    def lanes(h):
-        return slice(h * WIDTH, (h + 1) * WIDTH)
-
-    core_copies = []
-    for h in range(CHUNKS):
-        copy = remote(own_body.at[:, lanes(h)], core_body.at[:, lanes(h)], core_sem.at[h], chan_peer(HOP_CORE))
-        copy.start()
-        core_copies.append(copy)
-    end = own_body.at[:, (TILES - 1) * LANES :]
-    tail_copies = [
-        remote(end, own_tail, tail_sem.at[0], (c, later)),
-        remote(end, core_tail, tail_sem.at[1], (other, later)),
-    ]
-    for copy in tail_copies:
-        copy.start()
-
-    body_hops, tail_hops = {}, {}
-    finals = {"A": len(MESSAGES), "B": len(MESSAGES) + 1, "F": len(MESSAGES) + 2}
-
-    def next_slot(name, stage):
-        following = [i for i, (s, n) in enumerate(MESSAGES) if n == name and s > stage]
-        return following[0] if following else finals[name]
-
-    def send_body(at, h):
-        if at < len(MESSAGES):
-            stage, name = MESSAGES[at]
-            src = core_body if (stage, name) == FIRST_F else hold.at[at]
-            copy = remote(
-                src.at[:, lanes(h)], hop_body.at[at, :, lanes(h)], body_sem.at[at, h],
-                chan_peer(dict(STAGES[stage])[name]),
-            )
-            copy.start()
-            body_hops[at, h] = copy
-
-    def send_tail(at):
-        if at < len(MESSAGES):
-            stage, name = MESSAGES[at]
-            copy = remote(
-                hold_tail.at[at], hop_tail.at[at], htail_sem.at[at], chan_peer(dict(STAGES[stage])[name])
-            )
-            copy.start()
-            tail_hops[at] = copy
-
-    def hop_bodies(stage):
-        for h in range(CHUNKS):
-            for name, hop in STAGES[stage]:
-                at = MESSAGES.index((stage, name))
-                slot = next_slot(name, stage)
-                body_hops[at, h].wait_recv()
-                value = hop_body[at, :, lanes(h)]
-                if name != "F":
-                    value = jnp.where(flag(masks[name], hop), value, hold[at, :, lanes(h)])
-                hold[slot, :, lanes(h)] = value
-                send_body(slot, h)
-
-    def hop_tails(stage):
-        for name, hop in STAGES[stage]:
-            at = MESSAGES.index((stage, name))
-            slot = next_slot(name, stage)
-            tail_hops[at].wait_recv()
-            value = hop_tail[at]
-            if name != "F":
-                value = jnp.where(flag(masks[name], hop), value, hold_tail[at])
-            hold_tail[slot] = value
-            send_tail(slot)
+    body = Stream(STAGES, pieces, flags, hold, hop_body, body_sem, by_hop)
+    tail = Stream(STAGES, [slice(0, LANES)], flags, hold_tail, hop_tail, tail_sem, by_hop)
+
+    def choose(name, values):
+        core, z1 = flags[name, HOP_CORE], flags[name, HOP_Z1]
+        return jnp.where(z1, jnp.where(core, values[3], values[2]), jnp.where(core, values[1], values[0]))
 
     def spectra(blocks):
         filtered = []
-        for body, tail in blocks:
-            tiles = [body[:, j * LANES : (j + 1) * LANES] for j in range(TILES)]
+        for block, before_it in blocks:
+            tiles = [block[:, j * LANES : (j + 1) * LANES] for j in range(TILES)]
             now = jnp.concatenate(tiles, 0)
-            before = jnp.concatenate([tail] + tiles[:-1], 0)
+            before = jnp.concatenate([before_it] + tiles[:-1], 0)
             both = jnp.dot(jnp.concatenate([before, now], 1), band[...], preferred_element_type=F32)
             filtered.append(both[:, :LANES] + both[:, LANES:])
         y = []
@@ -311,7 +306,10 @@
 
         lax.fori_loop(0, CH, step, 0)
         lagged = jnp.dot(cross[...], lag_mat[...], preferred_element_type=F32)
-        parts[slot] = lagged.astype(BF16).reshape(TM, 32, 256)
+        parts[slot, :, :32, :] = lagged[:, :LANES].astype(BF16).reshape(TM, 32, LANES)
+        last = lagged[:, LANES:].reshape(TM, 2, CH, LANES)
+        lane0 = lax.broadcasted_iota(jnp.int32, (TM, CH, LANES), 2) == 0
+        parts[slot, :, 32:, :] = jnp.where(lane0, last[:, 0], last[:, 1]).astype(BF16)
 
     reduce_copies = []
 
@@ -326,57 +324,60 @@
             copy.start()
             reduce_copies.append(copy)
 
-    for h in range(CHUNKS):
-        core_copies[h].wait_recv()
-        mine, theirs = own_body[:, lanes(h)], core_body[:, lanes(h)]
+    for load in loads[2:]:
+        load.wait()
+    for h, piece in enumerate(pieces):
+        for copy in first_copies[h]:
+            copy.wait_recv()
+        blocks = [own[:, piece]] + [near_body[k, :, piece] for k in range(len(NEAR))]
         for n in "AB":
-            at = next_slot(n, -1)
-            hold[at, :, lanes(h)] = jnp.where(flag(masks[n], HOP_CORE), theirs, mine)
-            send_body(at, h)
-        send_body(next_slot("F", -1), h)
-    for load in loads[3:]:
-        load.wait()
-
-    hop_bodies(0)
-    for copy in tail_copies:
+            hold[body.slot(n), :, piece] = choose(n, blocks)
+            body.leave(body.slot(n), h)
+        body.leave(body.slot("F"), h, near_body.at[0])
+
+    for copy in near_copies[:2]:
         copy.wait_recv()
-    mine = jnp.where(t == 0, jnp.zeros_like(own_tail), own_tail[...])
-    theirs = jnp.where(t == 0, jnp.zeros_like(core_tail), core_tail[...])
-    for n in "ABF":
-        at = next_slot(n, -1)
-        hold_tail[at] = theirs if n == "F" else jnp.where(flag(masks[n], HOP_CORE), theirs, mine)
-        send_tail(at)
-    spec = spectra([(own_body[...], mine), (core_body[...], theirs)])
+    ends = [jnp.where(t == 0, jnp.zeros((CH, LANES), BF16), near_tails[k]) for k in range(2)]
+    hold_tail[tail.slot("F")] = ends[1]
+    tail.leave(tail.slot("F"), 0)
+    spec = spectra([(own[...], ends[0]), (near_body[0], ends[1])])
     for g in range(GROUPS):
         xr[g], xi[g] = spec[g][0][:32], spec[g][1][:32]
+
+    for copy in near_copies[2:]:
+        copy.wait_recv()
+    ends += [jnp.where(t == 0, jnp.zeros((CH, LANES), BF16), near_tails[k]) for k in (2, 3)]
+    for n in "AB":
+        hold_tail[tail.slot(n)] = choose(n, ends)
+        tail.leave(tail.slot(n), 0)
     keep_partner(spec, 0)
     correlate(0)
-    hop_tails(0)
-    hop_bodies(1)
+    body.hop(0)
     keep_partner(spec, 1)
     correlate(1)
     send_parts(0, 2)
-    hop_tails(1)
-    hop_bodies(2)
-    hop_tails(2)
-    spec = spectra([(hold[finals["F"]], hold_tail[finals["F"]])])
+    tail.hop(0)
+    body.hop(1)
+    tail.hop(1)
+    body.hop(2)
+    tail.hop(2)
+    spec = spectra([(hold[body.finals["F"]], hold_tail[tail.finals["F"]])])
     keep_partner(spec, 0)
     correlate(2)
     send_parts(2, 1)
-    hop_bodies(3)
-    hop_tails(3)
-    hop_bodies(4)
-    hop_tails(4)
-    spec = spectra([(hold[finals[n]], hold_tail[finals[n]]) for n in "AB"])
-    for i in range(2):
-        keep_partner(spec, i)
-        correlate(3 + i)
-        send_parts(3 + i, 1)
-
-    for copy in [*core_copies, *tail_copies, *body_hops.values(), *tail_hops.values()]:
+    body.hop(3)
+    tail.hop(3)
+    spec = spectra([(hold[body.finals[n]], hold_tail[tail.finals[n]]) for n in "AB"])
+    for k in range(2):
+        keep_partner(spec, k)
+        correlate(3 + k)
+        send_parts(3 + k, 1)
+
+    for copy in [*sum(first_copies, []), *near_copies, *body.copies.values(), *tail.copies.values()]:
         copy.wait_send()
     for copy in reduce_copies:
         copy.wait_recv()
+
     for slot in range(5):
         acc = parts[slot, t].astype(F32)
         for d in range(1, TM):
@@ -389,11 +390,16 @@
 def hand_out(plan, sums, self_out, pair_out):
     p = [plan[r] for r in range(ROUNDS)]
     first = jnp.where(known(p[0]), jnp.where(known(p[1]), p[2], p[1]), p[0])
-    shaped = lambda i: sums[i][:, :LAGS].reshape(2, CH, LAGS)
-    self_out[...] = shaped(0)
+
+    def write(out, slot):
+        for a in range(2):
+            out[a, :, :LANES] = sums[slot, a * CH : (a + 1) * CH, :]
+            out[a, :, LANES:] = sums[slot, 32:, a : a + 1]
+
+    write(self_out, 0)
     for r in range(ROUNDS):
         slot = jnp.where(p[r] == 1, 1, jnp.where(p[r] == 63, 2, jnp.where(p[r] == first, 3, 4)))
-        pair_out[r] = shaped(slot)
+        write(pair_out.at[r], slot)
 
 
 def on_device(samples, fir_taps, plan):
@@ -401,13 +407,12 @@
     lag_mat = lag_table()
     vmem = pl.BlockSpec(memory_space=pltpu.VMEM)
     anywhere = pl.BlockSpec(memory_space=pl.ANY)
-    n = len(MESSAGES)
-    slots = n + 3
+    n = len(messages(STAGES))
     dma = pltpu.SemaphoreType.DMA
     taps = fir_taps.reshape(1, -1)
     sums = pl.pallas_call(
         kernel,
-        out_shape=jax.ShapeDtypeStruct((5, 32, 256), F32),
+        out_shape=jax.ShapeDtypeStruct((5, ROWS, LANES), F32),
         in_specs=[anywhere] * 6,
         out_specs=vmem,
         scratch_shapes=[
@@ -418,13 +423,12 @@
             pltpu.VMEM(dft_low.shape, BF16),
             pltpu.VMEM(lag_mat.shape, BF16),
             pltpu.VMEM((CH, 2048), BF16),
-            pltpu.VMEM((CH, 2048), BF16),
+            pltpu.VMEM((len(NEAR), CH, 2048), BF16),
             pltpu.VMEM((n, CH, 2048), BF16),
-            pltpu.VMEM((slots, CH, 2048), BF16),
-            pltpu.VMEM((CH, LANES), BF16),
-            pltpu.VMEM((CH, LANES), BF16),
+            pltpu.VMEM((n + 3, CH, 2048), BF16),
+            pltpu.VMEM((len(NEAR) + 1, CH, LANES), BF16),
             pltpu.VMEM((n, CH, LANES), BF16),
-            pltpu.VMEM((slots, CH, LANES), BF16),
+            pltpu.VMEM((n + 3, CH, LANES), BF16),
             pltpu.VMEM((256, 256), BF16),
             pltpu.VMEM((GROUPS, 32, LANES), F32),
             pltpu.VMEM((GROUPS, 32, LANES), F32),
@@ -432,13 +436,13 @@
             pltpu.VMEM((GROUPS, 32, LANES), F32),
             pltpu.VMEM((GROUPS, 32, LANES), F32),
             pltpu.VMEM((256, GROUPS * 256), BF16),
-            pltpu.VMEM((5, TM, 32, 256), BF16),
-            pltpu.VMEM((TM - 1, 5, 32, 256), BF16),
+            pltpu.VMEM((5, TM, ROWS, LANES), BF16),
+            pltpu.VMEM((TM - 1, 5, ROWS, LANES), BF16),
             dma((6,)),
-            dma((CHUNKS, 2)),
-            dma((2, 2)),
+            dma((CHUNKS, len(NEAR), 2)),
+            dma((len(NEAR) + 1, 2)),
             dma((n, CHUNKS, 2)),
-            dma((n, 2)),
+            dma((n, 1, 2)),
             dma((5, TM - 1, 2)),
         ],
         compiler_params=pltpu.CompilerParams(

time: 49.2 us -> 47.1 us (0.957)
  the two profiles are of different devices: /device:TPU:8 before, /device:TPU:2 now
where the time goes in v3:
time: 47.1 us; the launch traced here: 47 us
  Pallas kernels  46.3 us (98%)
  between operations  0.64 us (1%)
    pallas_call x1, Pallas kernels, on_device(): pl.pallas_call(kernel, out_shape=jax.ShapeDtypeStruct((5, ROWS, LANES), F...  44.7 us
    pallas_call x1, Pallas kernels, on_device(): pl.pallas_call(hand_out, out_shape=(jax.ShapeDtypeStruct((2, CH, LAGS), F...  1.66 us

profile of v3, /device:TPU:2, one launch (start us, length us, event | category | flops | bytes accessed | tf_op | source)
XLA Modules:
  0.0 47.0 jit_solution(928844472987617118)
XLA Ops:
  0.6 44.7 %correlate_blocks.1.sums = f32[5,48,128]{2,1,0:T(8,128)} custom-call(s32[4]{0:T(128)} %plan.1, bf16[16,2048]{1,0:T(8,128)(2,1)} %samples.1, f32[1,96]{1,0:T(1,128)} %bitcast.1, bf16[4,256,256]{2,1,0:T(8,128)(2,1)} %constant.6.clone.dft_high_in, bf16[4,256,256]{2,1,0:T(8,128)(2,1)} %constant.7.clone.dft_low_in, bf16[1024,256]{1,0:T(8,128)(2,1)} %constant.8.clone.lag_in), custom_call_target="tpu_custom_call" | custom-call | flops 1000000000 | bytes 4000000 | tf_op jit(solution)/shard_map/correlate_blocks/pallas_call | solution.py:413
  45.3 1.7 %hand_out_rounds.1 = (f32[2,16,129]{2,1,0:T(8,128)}, f32[4,2,16,129]{3,2,1,0:T(8,128)}) custom-call(s32[4]{0:T(128)} %plan.1, f32[5,48,128]{2,1,0:T(8,128)} %correlate_blocks.1.sums), custom_call_target="tpu_custom_call" | custom-call | bytes 500000 | tf_op jit(solution)/shard_map/hand_out_rounds/pallas_call | solution.py:454

commit v4 on v3

--- a/solution.py
+++ b/solution.py
@@ -155,8 +155,6 @@
             (dft_high_in, dft_high), (dft_low_in, dft_low), (lag_in, lag_mat),
         ))
     ]
-    for load in loads:
-        load.start()
     pl.semaphore_wait(barrier, len(greeted))
 
     def remote(src, dst, sem, device):
@@ -178,8 +176,10 @@
         remote(end, near_tails.at[k], near_sem.at[k], (chan_peer(hop)[0], later))
         for k, hop in enumerate((0,) + NEAR)
     ]
-    for copy in [*first_copies[0], *near_copies, *sum(first_copies[1:], [])]:
+    for copy in [*first_copies[0][::-1], *near_copies, *[x for row in first_copies[1:] for x in row[::-1]]]:
         copy.start()
+    for load in loads:
+        load.start()
 
     loads[0].wait()
     loads[1].wait()
@@ -304,17 +304,17 @@
                 cross[where, g * 256 + LANES : (g + 1) * 256] = sum_im.astype(BF16)
             return carry
 
-        lax.fori_loop(0, CH, step, 0)
+        lax.fori_loop(0, CH, step, 0, unroll=4)
         lagged = jnp.dot(cross[...], lag_mat[...], preferred_element_type=F32)
         parts[slot, :, :32, :] = lagged[:, :LANES].astype(BF16).reshape(TM, 32, LANES)
         last = lagged[:, LANES:].reshape(TM, 2, CH, LANES)
         lane0 = lax.broadcasted_iota(jnp.int32, (TM, CH, LANES), 2) == 0
         parts[slot, :, 32:, :] = jnp.where(lane0, last[:, 0], last[:, 1]).astype(BF16)
 
-    reduce_copies = []
+    reduce_copies = {slot: [] for slot in range(5)}
 
     def send_parts(first, count):
-        for d in range(1, TM):
+        for d in (6, 5, 7, 2, 4, 1, 3):
             copy = remote(
                 parts.at[pl.ds(first, count), lax.bitwise_xor(t, jnp.int32(d))],
                 inbox.at[d - 1, pl.ds(first, count)],
@@ -322,7 +322,7 @@
                 tm_peer(d),
             )
             copy.start()
-            reduce_copies.append(copy)
+            reduce_copies[first].append(copy)
 
     for load in loads[2:]:
         load.wait()
@@ -373,17 +373,15 @@
         correlate(3 + k)
         send_parts(3 + k, 1)
 
-    for copy in [*sum(first_copies, []), *near_copies, *body.copies.values(), *tail.copies.values()]:
-        copy.wait_send()
-    for copy in reduce_copies:
-        copy.wait_recv()
-
     for slot in range(5):
+        for copy in reduce_copies[slot]:
+            copy.wait_recv()
         acc = parts[slot, t].astype(F32)
         for d in range(1, TM):
             acc = acc + inbox[d - 1, slot].astype(F32)
         sums[slot] = acc
-    for copy in reduce_copies:
+    reduced = [copy for copies in reduce_copies.values() for copy in copies]
+    for copy in [*sum(first_copies, []), *near_copies, *body.copies.values(), *tail.copies.values(), *reduced]:
         copy.wait_send()
 
 

time: 47.1 us -> 46.5 us (0.987)
  Pallas kernels: 46.3 us -> 45.7 us
    pallas_call x1, Pallas kernels: 44.7 us -> 44.1 us  [on_device(): pl.pallas_call(kernel, out_shape=jax.ShapeDtypeStruct((5, ROWS, LANES), F...]
where the time goes in v4:
time: 46.5 us; the launch traced here: 46.4 us
  Pallas kernels  45.7 us (98%)
  between operations  0.64 us (1%)
    pallas_call x1, Pallas kernels, on_device(): pl.pallas_call(kernel, out_shape=jax.ShapeDtypeStruct((5, ROWS, LANES), F...  44.1 us
    pallas_call x1, Pallas kernels, on_device(): pl.pallas_call(hand_out, out_shape=(jax.ShapeDtypeStruct((2, CH, LAGS), F...  1.66 us

profile of v4, /device:TPU:2, one launch (start us, length us, event | category | flops | bytes accessed | tf_op | source)
XLA Modules:
  0.0 46.4 jit_solution(11400971369568793014)
XLA Ops:
  0.6 44.1 %correlate_blocks.1.sums = f32[5,48,128]{2,1,0:T(8,128)} custom-call(s32[4]{0:T(128)} %plan.1, bf16[16,2048]{1,0:T(8,128)(2,1)} %samples.1, f32[1,96]{1,0:T(1,128)} %bitcast.1, bf16[4,256,256]{2,1,0:T(8,128)(2,1)} %constant.6.clone.dft_high_in, bf16[4,256,256]{2,1,0:T(8,128)(2,1)} %constant.7.clone.dft_low_in, bf16[1024,256]{1,0:T(8,128)(2,1)} %constant.8.clone.lag_in), custom_call_target="tpu_custom_call" | custom-call | flops 1000000000 | bytes 4000000 | tf_op jit(solution)/shard_map/correlate_blocks/pallas_call | solution.py:411
  44.7 1.7 %hand_out_rounds.1 = (f32[2,16,129]{2,1,0:T(8,128)}, f32[4,2,16,129]{3,2,1,0:T(8,128)}) custom-call(s32[4]{0:T(128)} %plan.1, f32[5,48,128]{2,1,0:T(8,128)} %correlate_blocks.1.sums), custom_call_target="tpu_custom_call" | custom-call | bytes 500000 | tf_op jit(solution)/shard_map/hand_out_rounds/pallas_call | solution.py:452

commit v5 on v4

--- a/solution.py
+++ b/solution.py
@@ -25,7 +25,7 @@
 ROWS = 48
 GROUPS = 4
 HOP_CORE, HOP_Z1, HOP_Z2, HOP_Z6, HOP_Z7, HOP_Y1, HOP_Y3 = 1, 2, 4, 12, 14, 16, 48
-CHAN_HOPS = (HOP_CORE, HOP_Z1, HOP_Z1 ^ HOP_CORE, HOP_Z2, HOP_Z6, HOP_Z7, HOP_Y1, HOP_Y3)
+CHAN_HOPS = (HOP_Z7, HOP_Z6, HOP_Y3, HOP_Y1, HOP_Z2, HOP_Z1, HOP_Z1 ^ HOP_CORE, HOP_CORE)
 STAGES = (
     (("A", HOP_Z2), ("B", HOP_Y3), ("F", HOP_Z7)),
     (("A", HOP_Z6), ("B", HOP_Y1), ("F", HOP_Y3)),

time: 46.5 us -> 46.5 us (level)
  no operation moved by 1% of the time
where the time goes in v5:
time: 46.5 us; the launch traced here: 46.4 us
  Pallas kernels  45.7 us (98%)
  between operations  0.64 us (1%)
    pallas_call x1, Pallas kernels, on_device(): pl.pallas_call(kernel, out_shape=jax.ShapeDtypeStruct((5, ROWS, LANES), F...  44.1 us
    pallas_call x1, Pallas kernels, on_device(): pl.pallas_call(hand_out, out_shape=(jax.ShapeDtypeStruct((2, CH, LAGS), F...  1.66 us

profile of v5, /device:TPU:2, one launch (start us, length us, event | category | flops | bytes accessed | tf_op | source)
XLA Modules:
  0.0 46.4 jit_solution(6482257788517432520)
XLA Ops:
  0.6 44.1 %correlate_blocks.1.sums = f32[5,48,128]{2,1,0:T(8,128)} custom-call(s32[4]{0:T(128)} %plan.1, bf16[16,2048]{1,0:T(8,128)(2,1)} %samples.1, f32[1,96]{1,0:T(1,128)} %bitcast.1, bf16[4,256,256]{2,1,0:T(8,128)(2,1)} %constant.6.clone.dft_high_in, bf16[4,256,256]{2,1,0:T(8,128)(2,1)} %constant.7.clone.dft_low_in, bf16[1024,256]{1,0:T(8,128)(2,1)} %constant.8.clone.lag_in), custom_call_target="tpu_custom_call" | custom-call | flops 1000000000 | bytes 4000000 | tf_op jit(solution)/shard_map/correlate_blocks/pallas_call | solution.py:411
  44.7 1.7 %hand_out_rounds.1 = (f32[2,16,129]{2,1,0:T(8,128)}, f32[4,2,16,129]{3,2,1,0:T(8,128)}) custom-call(s32[4]{0:T(128)} %plan.1, f32[5,48,128]{2,1,0:T(8,128)} %correlate_blocks.1.sums), custom_call_target="tpu_custom_call" | custom-call | bytes 500000 | tf_op jit(solution)/shard_map/hand_out_rounds/pallas_call | solution.py:452
